TPU v7x, 256 devices: a whole 4x4x8 slice. The times are simulated.
256 devices in a mesh: seq: 8 (over z_lo, core), tile: 32 (over y, z_hi, x).
Axes of the slice: x: 4, y: 4, z: 8 (z_hi: 2, z_lo: 4; z = z_hi * 4 + z_lo), core: 2. Of those that a mesh axis runs over, the one named last changes fastest.
Arguments:
- queries: bfloat16 [16384, 2048], P(('seq', 'tile')), may hold values from -9 to 9
- keys: bfloat16 [16384, 2048], P(('seq', 'tile')), may hold values from -9 to 9
- values: bfloat16 [16384, 2048], P(('seq', 'tile')), may hold values from -6 to 6
- w_final: bfloat16 [2048, 64], replicated, may hold values from -12 to 12
- w_in: bfloat16 [3, 3, 3, 16, 256], replicated, may hold values from -0.3125 to 0.3125
- b_in: float32 [256], replicated, may hold values from -3 to 3
- w_out: bfloat16 [3, 3, 3, 256, 256], replicated, may hold values from -0.078125 to 0.078125
- b_out: float32 [256], replicated, may hold values from -3 to 3
Outputs:
- decoded: bfloat16 [16, 128, 128, 256], P('seq', None, 'tile')
All inputs are finite; a program needn't handle non-finite values.
Results may differ from a plain program's by a relative error of at most 0.018.
Values may be sent and summed in bfloat16 or wider, within the bound.
No kernel may reach another device: no remote copies, remote signals or barrier semaphores. Data moves between devices by JAX's collectives and lax.ppermute only.
A program may use at most 64 MiB of HBM per device.

v0:
```python
import functools
import math

import jax
import jax.numpy as jnp
from jax import lax
from jax.experimental import pallas as pl
from jax.experimental.pallas import tpu as pltpu
from jax.sharding import Mesh, PartitionSpec as P

AXES = ("zl", "core", "y", "zh", "x")
SIZES = (4, 2, 4, 2, 4)
PLANE = ("y", "x")
STACK = ("zl", "core", "zh")
RING = ("zl", "zh")

HEADS = 16
HD = 128
PW = 64
CH = 256
TOK = 64
MSG = 96
PLANE_TOK = 1024
SCALE = math.log2(math.e) / math.sqrt(HD)
BF = jnp.bfloat16
F32 = jnp.float32


def params(mib):
    return pltpu.CompilerParams(vmem_limit_bytes=mib * 2**20)


def cost(flops, moved):
    return pl.CostEstimate(flops=flops, bytes_accessed=moved, transcendentals=0)


def pack_kernel(q_hbm, k_hbm, v_hbm, w_hbm, out_ref, q_ref, k_ref, v_ref, w_ref, sems):
    moves = [
        pltpu.make_async_copy(source, target, sems.at[i])
        for i, (source, target) in enumerate(
            ((v_hbm, v_ref), (w_hbm, w_ref), (k_hbm, k_ref), (q_hbm, q_ref))
        )
    ]
    for move in moves:
        move.start()
    for move in moves[:2]:
        move.wait()
    for head in range(HEADS):
        lanes = pl.ds(head * HD, HD)
        small = lax.dot_general(
            v_ref[:, lanes], w_ref[:, lanes], (((1,), (1,)), ((), ())), preferred_element_type=F32
        )
        packed = jnp.concatenate([small[: TOK // 2], small[TOK // 2 :]], axis=1)
        out_ref[head, TOK:MSG] = packed.astype(BF)
    for move in moves[2:]:
        move.wait()
    for head in range(HEADS):
        lanes = pl.ds(head * HD, HD)
        out_ref[head, 0:TOK] = k_ref[:, lanes]
        out_ref[head, MSG : MSG + TOK] = q_ref[:, lanes]


def pack(queries, keys, values, w_final):
    return pl.pallas_call(
        pack_kernel,
        in_specs=[pl.BlockSpec(memory_space=pl.ANY)] * 4,
        out_shape=jax.ShapeDtypeStruct((HEADS, MSG + TOK, HD), BF),
        scratch_shapes=[pltpu.VMEM((TOK, HEADS * HD), BF)] * 3
        + [pltpu.VMEM((PW, HEADS * HD), BF), pltpu.SemaphoreType.DMA((4,))],
        compiler_params=params(60),
        cost_estimate=cost(2 * TOK * HEADS * HD * PW, 2**20),
        name="pack",
    )(queries, keys, values, w_final.T)


def attend_kernel(first, *refs):
    q_ref, kv_ref = refs[:2]
    old_ref = None if first else refs[2]
    new_ref, trial_ref, peak_ref = refs[-3:]
    sources = kv_ref.shape[0]

    def chunk(begin, count):
        rows = count * TOK
        keys = kv_ref[pl.ds(begin, count), 0:TOK, :].reshape(rows, HD)
        packed = kv_ref[pl.ds(begin, count), TOK:MSG, :]
        small = jnp.concatenate([packed[:, :, :PW], packed[:, :, PW:]], axis=1).reshape(rows, PW)
        return keys, jnp.concatenate([small, jnp.ones_like(small)], axis=1)

    def scores(keys, q):
        s = lax.dot_general(keys, q, (((1,), (1,)), ((), ())), preferred_element_type=F32)
        return s.reshape(s.shape[0] // 8, 8, s.shape[1]) * SCALE

    def weighted(s, shift, wide):
        p = jnp.exp2(s - shift[None])
        p = p.reshape(s.shape[0] * 8, s.shape[2]).astype(BF)
        u = lax.dot_general(wide, p, (((0,), (0,)), ((), ())), preferred_element_type=F32)
        return u[PW : PW + 8], u[:PW]

    def raise_peak(side, count):
        def more(i, _):
            s = scores(chunk(2 * i, 2)[0], q_ref[side])
            top = jnp.max(jnp.max(s, axis=0), axis=0, keepdims=True)
            peak_ref[...] = jnp.maximum(peak_ref[...], top)
            return 0

        lax.fori_loop(0, count // 2, more, 0)

    def attempt(side, largest):
        q = q_ref[side]
        if first:
            peak_ref[...] = jnp.full(peak_ref.shape, -jnp.inf, F32)
            raise_peak(side, 8)
            shift = peak_ref[...]
            total = jnp.zeros_like(shift)
            summed = jnp.zeros((PW, shift.shape[1]), F32)
        else:
            summed = old_ref[side, 0:PW]
            total = old_ref[side, PW : PW + 8]
            shift = old_ref[side, PW + 8 : PW + 16]
        fresh = jnp.zeros_like(total)
        for begin in range(0, sources, 8):
            keys, wide = chunk(begin, 8)
            t, u = weighted(scores(keys, q), shift, wide)
            fresh = fresh + t
            summed = summed + u
        trial_ref[side, 0:PW] = summed
        trial_ref[side, PW : PW + 8] = total + fresh
        trial_ref[side, PW + 8 : PW + 16] = shift
        return jnp.maximum(largest, jnp.max(fresh))

    largest = lax.fori_loop(0, q_ref.shape[0], attempt, jnp.float32(0))
    within = largest <= 2.0**100

    @pl.when(within)
    def _():
        new_ref[...] = trial_ref[...]

    @pl.when(jnp.logical_not(within))
    def _():
        def again(side, _):
            if first:
                new_ref[side] = jnp.zeros(new_ref.shape[1:], F32)
                shift = trial_ref[side, PW + 8 : PW + 16]
            else:
                new_ref[side] = old_ref[side]
                shift = new_ref[side, PW + 8 : PW + 16]
            peak_ref[...] = shift
            raise_peak(side, sources)
            top = peak_ref[...]
            shrink = jnp.exp2(shift - top)
            new_ref[side, 0:PW] = new_ref[side, 0:PW] * shrink[0:1]
            new_ref[side, PW : PW + 8] = new_ref[side, PW : PW + 8] * shrink
            new_ref[side, PW + 8 : PW + 16] = top

            def more(i, _):
                keys, wide = chunk(2 * i, 2)
                t, u = weighted(scores(keys, q_ref[side]), top, wide)
                new_ref[side, 0:PW] += u
                new_ref[side, PW : PW + 8] += t
                return 0

            return lax.fori_loop(0, sources // 2, more, 0)

        lax.fori_loop(0, q_ref.shape[0], again, 0)


def attend(queries, message, state):
    first = state is None
    operands = [queries, message] + ([] if first else [state])
    rows = message.shape[0] * TOK
    sides = queries.shape[0]
    return pl.pallas_call(
        functools.partial(attend_kernel, first),
        out_shape=jax.ShapeDtypeStruct((sides, PW + 16, PLANE_TOK), F32),
        scratch_shapes=[
            pltpu.VMEM((sides, PW + 16, PLANE_TOK), F32),
            pltpu.VMEM((8, PLANE_TOK), F32),
        ],
        input_output_aliases={} if first else {2: 0},
        compiler_params=params(20),
        cost_estimate=cost(2 * sides * PLANE_TOK * rows * 2 * HD, sides * 2**20),
        name="attend",
    )(*operands)


def join_kernel(mine_ref, other_ref, out_ref, rows_ref):
    top = jnp.maximum(mine_ref[PW + 8 : PW + 16], other_ref[PW + 8 : PW + 16])
    one = jnp.exp2(mine_ref[PW + 8 : PW + 16] - top)
    two = jnp.exp2(other_ref[PW + 8 : PW + 16] - top)
    total = mine_ref[PW : PW + 8] * one + other_ref[PW : PW + 8] * two
    summed = mine_ref[0:PW] * one[0:1] + other_ref[0:PW] * two[0:1]
    share = summed / total[0:1]
    rows_ref[:, 0:PW] = jnp.transpose(share)
    none = jnp.zeros((32, PW), F32)
    columns = [rows_ref[pl.ds(c, 32, stride=32), 0:PW] for c in range(32)]

    def column(c):
        return columns[c] if 0 <= c < 32 else none

    for y in range(4):
        for x in range(4):
            for j in range(3):
                c = y * 8 + x - 1 + j
                both = jnp.concatenate([column(c), column(c + 4)], axis=1)
                out_ref[y * 4 + x, j] = both.astype(BF)


def join(mine, other):
    return pl.pallas_call(
        join_kernel,
        out_shape=jax.ShapeDtypeStruct((16, 3, 32, 2 * PW), BF),
        scratch_shapes=[pltpu.VMEM((PLANE_TOK, 2 * PW), F32)],
        compiler_params=params(24),
        cost_estimate=cost(2**20, 2**20),
        name="join",
    )(mine, other)


def patch_kernel(in_ref, out_ref):
    total = in_ref[0].astype(F32)
    for head in range(1, HEADS):
        total = total + in_ref[head].astype(F32)
    for strip in range(2):
        part = total[:, :, strip * PW : (strip + 1) * PW]
        flat = jnp.concatenate([part[:, 0:16], part[:, 16:32]], axis=2).astype(BF)
        for group in range(4):
            out_ref[2 * group + strip] = flat


def patches(parts):
    return pl.pallas_call(
        patch_kernel,
        out_shape=jax.ShapeDtypeStruct((8, 3, 16, 2 * PW), BF),
        compiler_params=params(24),
        cost_estimate=cost(2**19, 2**19),
        name="patch_sum",
    )(parts)


def spread_w_in(w_ref, w1_ref):
    none = jnp.zeros((16, CH), BF)
    for a in range(2):
        for b in range(2):
            for near in range(4):
                for beside in range(4):
                    dy, dx = near - 1 + a, beside - 1 + b
                    place = ((near // 2) * 2 + beside // 2) * PW + ((near % 2) * 2 + beside % 2) * 16
                    for dt in range(3):
                        known = 0 <= dy < 3 and 0 <= dx < 3
                        tap = w_ref[dt, dy, dx] if known else none
                        rows = pl.ds(dt * 4 * PW + place, 16)
                        w1_ref[a, rows, b * CH : (b + 1) * CH] = tap


PICKS = {(0, 0): (0,), (0, 1): (1, 2), (1, 0): (0, 1), (1, 1): (2,)}


def upsampled_conv(w_ref, act_ref, sum_ref):
    def one(dt, _):
        for p in range(2):
            totals = [None, None]
            for i in range(2):
                rows = []
                for dx in range(3):
                    row = w_ref[dt, PICKS[p, i][0], dx].astype(F32)
                    for dy in PICKS[p, i][1:]:
                        row = row + w_ref[dt, dy, dx].astype(F32)
                    rows.append(row)
                for q in range(2):
                    for j in range(2):
                        tap = rows[PICKS[q, j][0]]
                        for dx in PICKS[q, j][1:]:
                            tap = tap + rows[dx]
                        blocks = []
                        for a in range(2):
                            view = act_ref[a + p + i, pl.ds(dt, 2), q + j : q + j + 2]
                            blocks.append(view.reshape(128, CH))
                        lhs = jnp.concatenate(blocks, axis=0)
                        part = jnp.dot(lhs, tap.astype(BF), preferred_element_type=F32)
                        totals[q] = part if totals[q] is None else totals[q] + part
            for q in range(2):
                sum_ref[2 * p + q] += totals[q]
        return 0

    sum_ref[...] = jnp.zeros(sum_ref.shape, F32)
    lax.fori_loop(0, 3, one, 0)


def decode_kernel(
    where_ref, own_ref, other_ref, w_in_ref, b1_ref, w_out_ref, b2_ref, out_ref, act_ref, w1_ref, sum_ref
):
    spread_w_in(w_in_ref, w1_ref)
    seq = where_ref[0]
    tile = where_ref[1]
    tokens = []
    for back in (2, 1, 0):
        chip = jnp.maximum(seq - back, 0) >> 1
        known = (seq >= back).astype(F32)
        in_ref = other_ref if back == 1 else own_ref
        halves = [in_ref[2 * chip + zh].astype(F32) * known for zh in range(2)]
        for frame in range(2):
            lanes = slice(frame * PW, (frame + 1) * PW)
            columns = []
            for j in range(3):
                pieces = []
                for high in range(2):
                    for zh in range(2):
                        pieces.append(halves[zh][j, high * 8 : (high + 1) * 8, lanes])
                columns.append(jnp.concatenate(pieces, axis=0))
            tokens.append(columns)
    blank = jnp.zeros((1, 2 * PW), F32)
    views = {}
    for frame in range(6):
        for side in range(2):
            both = jnp.concatenate([tokens[frame][side], tokens[frame][side + 1]], axis=1)
            views[frame, side, 0] = both.astype(BF)
            views[frame, side, -1] = jnp.concatenate([blank, both[:-1]], axis=0).astype(BF)
            views[frame, side, 1] = jnp.concatenate([both[1:], blank], axis=0).astype(BF)

    blank = jnp.zeros((1, CH), F32)
    first = {}
    for a in range(2):
        for side in range(2):
            rows = []
            for frame in range(4):
                row = []
                for dt in range(3):
                    for near in range(2):
                        row.append(views[frame + dt, side, a - 1 + near])
                rows.append(jnp.concatenate(row, axis=1))
            lhs = jnp.concatenate(rows, axis=0)
            got = jnp.dot(lhs, w1_ref[a], preferred_element_type=F32)
            for half in range(2):
                column = 2 * side + half
                b = 1 - half
                first[a, column] = (got[:, b * CH : (b + 1) * CH] + b1_ref[...]).astype(BF)

    for column in range(4):
        inside = 1.0
        if column == 0:
            inside = (tile > 0).astype(F32)
        if column == 3:
            inside = (tile < 31).astype(F32)
        for a in range(2):
            full = first[a, column].astype(F32)
            active = full / (1.0 + jnp.exp(-full))
            for frame in range(4):
                keep = inside * ((seq > 0).astype(F32) if frame < 2 else 1.0)
                part = active[frame * 32 : (frame + 1) * 32] * keep
                if a == 0:
                    act_ref[1, frame, column] = part.astype(BF)
                    act_ref[3, frame, column] = jnp.concatenate([part[1:], blank], 0).astype(BF)
                else:
                    act_ref[2, frame, column] = part.astype(BF)
                    act_ref[0, frame, column] = jnp.concatenate([blank, part[:-1]], 0).astype(BF)

    upsampled_conv(w_out_ref, act_ref, sum_ref)
    to = lax.broadcasted_iota(jnp.int32, (256, 128), 0)
    source = lax.broadcasted_iota(jnp.int32, (256, 128), 1)
    order = jnp.where((to & 7) * 32 + (to >> 3) == source, 1.0, 0.0).astype(BF)
    for frame in range(2):
        for a in range(2):
            for p in range(2):
                columns = []
                for x in range(4):
                    column, q = x // 2, x % 2
                    start = (a * 4 + frame * 2 + column) * 32
                    skip = first[a, column + 1][(frame + 2) * 32 : (frame + 3) * 32].astype(F32)
                    columns.append(skip + sum_ref[2 * p + q, start : start + 32] + b2_ref[...])
                stacked = jnp.concatenate(columns, axis=0).astype(BF)
                rows = jnp.dot(order, stacked, preferred_element_type=F32)
                out_ref[frame, :, 2 * a + p] = rows.reshape(32, 8, CH)[:, 0:4].astype(BF)


def decode(where, own, other, w_in, b_in, w_out, b_out):
    vmem = pl.BlockSpec(memory_space=pltpu.VMEM)
    return pl.pallas_call(
        decode_kernel,
        in_specs=[pl.BlockSpec(memory_space=pltpu.SMEM)] + [vmem] * 6,
        out_specs=vmem,
        out_shape=jax.ShapeDtypeStruct((2, 32, 4, 4, CH), BF),
        scratch_shapes=[
            pltpu.VMEM((4, 4, 4, 32, CH), BF),
            pltpu.VMEM((2, 12 * PW, 2 * CH), BF),
            pltpu.VMEM((4, 256, CH), F32),
        ],
        compiler_params=params(24),
        cost_estimate=cost(2 * 2**30, 10 * 2**20),
        name="decode",
    )(where, own, other, w_in, b_in.reshape(1, CH), w_out, b_out.reshape(1, CH))


def around():
    pairs = []
    for core, step in ((0, 1), (1, -1)):
        for z in range(8):
            to = (z + step) % 8
            pairs.append(((z % 4) * 4 + core * 2 + z // 4, (to % 4) * 4 + core * 2 + to // 4))
    return pairs


def swapped(value, axes):
    return lax.all_to_all(value, axes, split_axis=0, concat_axis=0, tiled=True)


def hop(value):
    return lax.ppermute(value, STACK, around())


def across(value):
    return lax.ppermute(value, "core", [(0, 1), (1, 0)])


def shards(queries, keys, values, w_final, w_in, b_in, w_out, b_out):
    seq = lax.axis_index(("zl", "core")).astype(jnp.int32)
    tile = lax.axis_index(("y", "zh", "x")).astype(jnp.int32)
    where = jnp.stack([seq, tile])
    mixed = swapped(pack(queries, keys, values, w_final), PLANE)
    mine = mixed[:, 0:MSG]
    own_q = mixed[:, MSG:].reshape(PLANE_TOK, HD)
    both_q = jnp.stack([own_q, across(own_q)])
    state = attend(both_q, mine, None)
    coming = [hop(mine), hop(across(mine))]
    for step in range(6):
        message, state, where = lax.optimization_barrier((coming.pop(0), state, where))
        if step < 5:
            coming.append(hop(message))
        state = attend(both_q, message, state)
    message, state = lax.optimization_barrier((coming.pop(0), state))
    theirs = attend(both_q[1:2], message, state[1:2])
    theirs, kept_q, kept = lax.optimization_barrier((theirs, both_q[0:1], state[0:1]))
    crossed = across(theirs[0])
    ours = attend(kept_q, message, kept)
    parts = swapped(join(ours[0], crossed), PLANE)
    patch = swapped(patches(parts), RING)
    return decode(where, patch, across(patch), w_in, b_in, w_out, b_out).reshape(2, 128, 4, CH)


def solution(mesh):
    fine = Mesh(mesh.devices.reshape(SIZES), AXES)
    tokens = P(AXES, None)
    placed = (tokens, tokens, tokens, P(), P(), P(), P(), P())
    return jax.shard_map(
        shards,
        mesh=fine,
        in_specs=placed,
        out_specs=P(("zl", "core"), None, ("y", "zh", "x"), None),
        check_vma=False,
    )
```

profile of v0, /device:TPU:1, one launch (start us, length us, event | category | flops | bytes accessed | tf_op | source)
XLA Modules:
  0.0 107.8 jit_solution(1385520151936966292)
XLA Ops:
  0.0 2.3 %pack.1 = bf16[16,160,128]{2,1,0:T(8,128)(2,1)} custom-call(bf16[64,2048]{1,0:T(8,128)(2,1)} %q_hbm.1, bf16[64,2048]{1,0:T(8,128)(2,1)} %k_hbm.1, bf16[64,2048]{1,0:T(8,128)(2,1)} %v_hbm.1, bf16[64,2048]{1,0:T(8,128)(2,1)} %bitcast.20), custom_call_target="tpu_custom_call" | custom-call | flops 16777216 | bytes 1048576 | tf_op jit(solution)/shard_map/pack/pallas_call | solution.py:64
  2.3 19.4 %all_to_all.15 = bf16[16,160,128]{2,1,0:T(8,128)(2,1)S(1)} all-to-all(bf16[16,160,128]{2,1,0:T(8,128)(2,1)} %pack.1), channel_id=1, replica_groups=mesh['zl'=4,'core'=2,'y'=4,'zh'=2,'x'=4] {'y','x'}, dimensions={0} | all-to-all | bytes 1310720 | tf_op jit(solution)/shard_map/all_to_all | solution.py:403
  21.8 2.2 %collective-permute-start = (bf16[16,96,128]{2,1,0:T(8,128)(2,1)S(1)}, bf16[16,96,128]{2,1,0:T(8,128)(2,1)S(1)}, u32[]{:S(2)}, u32[]{:S(2)}) collective-permute-start(bf16[16,96,128]{2,1,0:T(8,128)(2,1)S(1)} %slice.16.refs_1_), channel_id=1, source_target_pairs={{0,32},{32,0},{1,33},{33,1},{2,34},{34,2},{3,35},{35,3},{4,36},{36... | collective-permute-start | bytes 1179656 | tf_op jit(solution)/shard_map/ppermute | solution.py:411
  24.0 0.1 collective-permute-start.2
  24.1 5.7 %collective-permute-start.3 = (bf16[16,96,128]{2,1,0:T(8,128)(2,1)S(1)}, bf16[16,96,128]{2,1,0:T(8,128)(2,1)S(1)}, u32[]{:S(2)}, u32[]{:S(2)}) collective-permute-start(bf16[16,96,128]{2,1,0:T(8,128)(2,1)S(1)} %slice.16.refs_1_), channel_id=1, source_target_pairs={{0,64},{64,128},{128,192},{192,4},{4,68},{68,132},{132,196},{196,0... | collective-permute-start | bytes 1179656 | tf_op jit(solution)/shard_map/ppermute | solution.py:407
  29.7 0.1 pad_add_fusion.where_ref
  29.8 0.0 collective-permute-done
  29.8 1.1 collective-permute-start.1
  30.9 0.0 collective-permute-done.2
  30.9 0.1 pad_maximum_fusion.refs_0_
  30.9 4.4 %attend.9.refs_2_ = f32[2,80,1024]{2,1,0:T(8,128)S(1)} custom-call(bf16[2,1024,128]{2,1,0:T(8,128)(2,1)S(1)} %pad_maximum_fusion.refs_0_, bf16[16,96,128]{2,1,0:T(8,128)(2,1)S(1)} %slice.16.refs_1_), custom_call_target="tpu_custom_call" | custom-call | flops 1073741824 | bytes 2097152 | tf_op jit(solution)/shard_map/attend/pallas_call | solution.py:172
  35.4 0.0 collective-permute-done.3.refs_1_
  35.4 11.3 %collective-permute-start.5 = (bf16[16,96,128]{2,1,0:T(8,128)(2,1)S(1)}, bf16[16,96,128]{2,1,0:T(8,128)(2,1)S(1)}, u32[]{:S(2)}, u32[]{:S(2)}) collective-permute-start(bf16[16,96,128]{2,1,0:T(8,128)(2,1)S(1)} %collective-permute-done.3.refs_1_), channel_id=1, source_target_pairs={{0,64},{64,128},{128,192},{192,4},{4,68},{68,132},{132,196},{196,0... | collective-permute-start | bytes 1179656 | tf_op jit(solution)/shard_map/ppermute | solution.py:407
  46.7 2.4 %attend.10.refs_2_ = f32[2,80,1024]{2,1,0:T(8,128)S(1)} custom-call(bf16[2,1024,128]{2,1,0:T(8,128)(2,1)S(1)} %pad_maximum_fusion.refs_0_, bf16[16,96,128]{2,1,0:T(8,128)(2,1)S(1)} %collective-permute-done.3.refs_1_, f32[2,80,1024]{2,1,0:T(8,128)S(1)} %attend.9.refs_2_), custom_call_target="tpu_custom_call", output_to_operand_aliasing={{}: (2, {})} | custom-call | flops 1073741824 | bytes 2097152 | tf_op jit(solution)/shard_map/attend/pallas_call | solution.py:172
  49.1 0.0 collective-permute-done.1.refs_1_
  49.1 0.8 collective-permute-start.4
  49.9 2.4 %attend.11.refs_2_ = f32[2,80,1024]{2,1,0:T(8,128)S(1)} custom-call(bf16[2,1024,128]{2,1,0:T(8,128)(2,1)S(1)} %pad_maximum_fusion.refs_0_, bf16[16,96,128]{2,1,0:T(8,128)(2,1)S(1)} %collective-permute-done.1.refs_1_, f32[2,80,1024]{2,1,0:T(8,128)S(1)} %attend.10.refs_2_), custom_call_target="tpu_custom_call", output_to_operand_aliasing={{}: (2, {})} | custom-call | flops 1073741824 | bytes 2097152 | tf_op jit(solution)/shard_map/attend/pallas_call | solution.py:172
  52.4 0.0 collective-permute-done.5.refs_1_
  52.4 2.2 %collective-permute-start.7 = (bf16[16,96,128]{2,1,0:T(8,128)(2,1)S(1)}, bf16[16,96,128]{2,1,0:T(8,128)(2,1)S(1)}, u32[]{:S(2)}, u32[]{:S(2)}) collective-permute-start(bf16[16,96,128]{2,1,0:T(8,128)(2,1)S(1)} %collective-permute-done.5.refs_1_), channel_id=1, source_target_pairs={{0,64},{64,128},{128,192},{192,4},{4,68},{68,132},{132,196},{196,0... | collective-permute-start | bytes 1179656 | tf_op jit(solution)/shard_map/ppermute | solution.py:407
  54.5 2.4 %attend.12.refs_2_ = f32[2,80,1024]{2,1,0:T(8,128)S(1)} custom-call(bf16[2,1024,128]{2,1,0:T(8,128)(2,1)S(1)} %pad_maximum_fusion.refs_0_, bf16[16,96,128]{2,1,0:T(8,128)(2,1)S(1)} %collective-permute-done.5.refs_1_, f32[2,80,1024]{2,1,0:T(8,128)S(1)} %attend.11.refs_2_), custom_call_target="tpu_custom_call", output_to_operand_aliasing={{}: (2, {})} | custom-call | flops 1073741824 | bytes 2097152 | tf_op jit(solution)/shard_map/attend/pallas_call | solution.py:172
  57.0 0.0 collective-permute-done.4.refs_1_
  57.0 1.8 %collective-permute-start.6 = (bf16[16,96,128]{2,1,0:T(8,128)(2,1)S(1)}, bf16[16,96,128]{2,1,0:T(8,128)(2,1)S(1)}, u32[]{:S(2)}, u32[]{:S(2)}) collective-permute-start(bf16[16,96,128]{2,1,0:T(8,128)(2,1)S(1)} %collective-permute-done.4.refs_1_), channel_id=1, source_target_pairs={{0,64},{64,128},{128,192},{192,4},{4,68},{68,132},{132,196},{196,0... | collective-permute-start | bytes 1179656 | tf_op jit(solution)/shard_map/ppermute | solution.py:407
  58.8 2.4 %attend.13.refs_2_ = f32[2,80,1024]{2,1,0:T(8,128)S(1)} custom-call(bf16[2,1024,128]{2,1,0:T(8,128)(2,1)S(1)} %pad_maximum_fusion.refs_0_, bf16[16,96,128]{2,1,0:T(8,128)(2,1)S(1)} %collective-permute-done.4.refs_1_, f32[2,80,1024]{2,1,0:T(8,128)S(1)} %attend.12.refs_2_), custom_call_target="tpu_custom_call", output_to_operand_aliasing={{}: (2, {})} | custom-call | flops 1073741824 | bytes 2097152 | tf_op jit(solution)/shard_map/attend/pallas_call | solution.py:172
  61.2 0.0 collective-permute-done.7.refs_1_
  61.2 1.8 %collective-permute-start.8 = (bf16[16,96,128]{2,1,0:T(8,128)(2,1)S(1)}, bf16[16,96,128]{2,1,0:T(8,128)(2,1)S(1)}, u32[]{:S(2)}, u32[]{:S(2)}) collective-permute-start(bf16[16,96,128]{2,1,0:T(8,128)(2,1)S(1)} %collective-permute-done.7.refs_1_), channel_id=1, source_target_pairs={{0,64},{64,128},{128,192},{192,4},{4,68},{68,132},{132,196},{196,0... | collective-permute-start | bytes 1179656 | tf_op jit(solution)/shard_map/ppermute | solution.py:407
  63.0 2.4 %attend.14.refs_2_ = f32[2,80,1024]{2,1,0:T(8,128)S(1)} custom-call(bf16[2,1024,128]{2,1,0:T(8,128)(2,1)S(1)} %pad_maximum_fusion.refs_0_, bf16[16,96,128]{2,1,0:T(8,128)(2,1)S(1)} %collective-permute-done.7.refs_1_, f32[2,80,1024]{2,1,0:T(8,128)S(1)} %attend.13.refs_2_), custom_call_target="tpu_custom_call", output_to_operand_aliasing={{}: (2, {})} | custom-call | flops 1073741824 | bytes 2097152 | tf_op jit(solution)/shard_map/attend/pallas_call | solution.py:172
  65.4 0.0 collective-permute-done.6.refs_1_
  65.4 2.4 %attend.15 = f32[2,80,1024]{2,1,0:T(8,128)S(1)} custom-call(bf16[2,1024,128]{2,1,0:T(8,128)(2,1)S(1)} %pad_maximum_fusion.refs_0_, bf16[16,96,128]{2,1,0:T(8,128)(2,1)S(1)} %collective-permute-done.6.refs_1_, f32[2,80,1024]{2,1,0:T(8,128)S(1)} %attend.14.refs_2_), custom_call_target="tpu_custom_call", output_to_operand_aliasing={{}: (2, {})} | custom-call | flops 1073741824 | bytes 2097152 | tf_op jit(solution)/shard_map/attend/pallas_call | solution.py:172
  67.8 0.9 collective-permute-done.8.refs_1_
  68.8 0.1 fusion
  68.8 0.0 copy-start
  68.9 0.0 copy-start.1
  68.9 0.0 copy-start.2
  68.9 0.0 copy-start.3
  68.9 1.2 %attend.16 = f32[1,80,1024]{2,1,0:T(8,128)S(1)} custom-call(bf16[1,1024,128]{2,1,0:T(8,128)(2,1)S(1)} %bitcast.17, bf16[16,96,128]{2,1,0:T(8,128)(2,1)S(1)} %collective-permute-done.8.refs_1_, f32[1,80,1024]{2,1,0:T(8,128)S(1)} %get-tuple-element.52.refs_2_), custom_call_target="tpu_custom_call", output_to_operand_aliasing={{}: (2, {})} | custom-call | flops 536870912 | bytes 1048576 | tf_op jit(solution)/shard_map/attend/pallas_call | solution.py:172
  70.1 2.0 %collective-permute-start.9 = (f32[80,1024]{1,0:T(8,128)S(1)}, f32[80,1024]{1,0:T(8,128)S(1)}, u32[]{:S(2)}, u32[]{:S(2)}) collective-permute-start(f32[80,1024]{1,0:T(8,128)S(1)} %bitcast.15), channel_id=1, source_target_pairs={{0,32},{32,0},{1,33},{33,1},{2,34},{34,2},{3,35},{35,3},{4,36},{36... | collective-permute-start | bytes 983048 | tf_op jit(solution)/shard_map/ppermute | solution.py:411
  72.1 1.2 %attend.17 = f32[1,80,1024]{2,1,0:T(8,128)S(1)} custom-call(bf16[1,1024,128]{2,1,0:T(8,128)(2,1)S(1)} %bitcast.14, bf16[16,96,128]{2,1,0:T(8,128)(2,1)S(1)} %collective-permute-done.8.refs_1_, f32[1,80,1024]{2,1,0:T(8,128)S(1)} %get-tuple-element.49.refs_2_), custom_call_target="tpu_custom_call", output_to_operand_aliasing={{}: (2, {})} | custom-call | flops 536870912 | bytes 1048576 | tf_op jit(solution)/shard_map/attend/pallas_call | solution.py:172
  73.4 0.0 collective-permute-done.9.other_ref
  73.4 0.5 join.1
  73.9 12.3 %all_to_all.16.in_ref = bf16[16,3,32,128]{3,2,1,0:T(8,128)(2,1)S(1)} all-to-all(bf16[16,3,32,128]{3,2,1,0:T(8,128)(2,1)S(1)} %join.1), channel_id=1, replica_groups=mesh['zl'=4,'core'=2,'y'=4,'zh'=2,'x'=4] {'y','x'}, dimensions={0} | all-to-all | bytes 786432 | tf_op jit(solution)/shard_map/all_to_all | solution.py:403
  86.2 0.1 patch_sum.1
  86.3 12.6 %all_to_all.17.own_ref = bf16[8,3,16,128]{3,2,1,0:T(8,128)(2,1)S(1)} all-to-all(bf16[8,3,16,128]{3,2,1,0:T(8,128)(2,1)S(1)} %patch_sum.1), channel_id=1, replica_groups=mesh['zl'=4,'core'=2,'y'=4,'zh'=2,'x'=4] {'zl','zh'}, dimensions={0} | all-to-all | bytes 196608 | tf_op jit(solution)/shard_map/all_to_all | solution.py:403
  99.0 3.0 %collective-permute-start.10 = (bf16[8,3,16,128]{3,2,1,0:T(8,128)(2,1)S(1)}, bf16[8,3,16,128]{3,2,1,0:T(8,128)(2,1)S(1)}, u32[]{:S(2)}, u32[]{:S(2)}) collective-permute-start(bf16[8,3,16,128]{3,2,1,0:T(8,128)(2,1)S(1)} %all_to_all.17.own_ref), channel_id=1, source_target_pairs={{0,32},{32,0},{1,33},{33,1},{2,34},{34,2},{3,35},{35,3},{4,36},{36... | collective-permute-start | bytes 294920 | tf_op jit(solution)/shard_map/ppermute | solution.py:411
  101.9 0.9 collective-permute-done.10.other_ref
  102.9 0.0 copy-done
  102.9 0.0 copy-done.1
  102.9 0.0 copy-done.2
  102.9 4.9 %decode.1 = bf16[2,32,4,4,256]{4,3,2,1,0:T(4,128)(2,1)} custom-call(s32[2]{0:T(128)S(1)} %pad_add_fusion.where_ref, bf16[8,3,16,128]{3,2,1,0:T(8,128)(2,1)S(1)} %all_to_all.17.own_ref, bf16[8,3,16,128]{3,2,1,0:T(8,128)(2,1)S(1)} %collective-permute-done.10.other_ref, bf16[3,3,3,16,256]{4,3,2,1,0:T(8,128)(2,1)S(1)} %copy-done.1, f32[1,256]{1,0:T(1,128)S(1)} %bitcast.18, ...), custom_call_target="tpu_custom_call" | custom-call | flops 2147483648 | bytes 10485760 | tf_op jit(solution)/shard_map/decode/pallas_call | solution.py:377
  (3 shorter events, 0.0 us)
Async XLA Ops:
  21.8 8.0 %collective-permute-start = (bf16[16,96,128]{2,1,0:T(8,128)(2,1)S(1)}, bf16[16,96,128]{2,1,0:T(8,128)(2,1)S(1)}, u32[]{:S(2)}, u32[]{:S(2)}) collective-permute-start(bf16[16,96,128]{2,1,0:T(8,128)(2,1)S(1)} %slice.16.refs_1_), channel_id=1, source_target_pairs={{0,32},{32,0},{1,33},{33,1},{2,34},{34,2},{3,35},{35,3},{4,36},{36... | collective-permute-start | bytes 1179656 | tf_op jit(solution)/shard_map/ppermute | solution.py:411
  24.0 6.9 %collective-permute-start.2 = (bf16[1024,128]{1,0:T(8,128)(2,1)S(1)}, bf16[1024,128]{1,0:T(8,128)(2,1)S(1)}, u32[]{:S(2)}, u32[]{:S(2)}) collective-permute-start(bf16[1024,128]{1,0:T(8,128)(2,1)S(1)} %bitcast.12), channel_id=1, source_target_pairs={{0,32},{32,0},{1,33},{33,1},{2,34},{34,2},{3,35},{35,3},{4,36},{36... | collective-permute-start | bytes 786440 | tf_op jit(solution)/shard_map/ppermute | solution.py:411
  24.1 11.3 %collective-permute-start.3 = (bf16[16,96,128]{2,1,0:T(8,128)(2,1)S(1)}, bf16[16,96,128]{2,1,0:T(8,128)(2,1)S(1)}, u32[]{:S(2)}, u32[]{:S(2)}) collective-permute-start(bf16[16,96,128]{2,1,0:T(8,128)(2,1)S(1)} %slice.16.refs_1_), channel_id=1, source_target_pairs={{0,64},{64,128},{128,192},{192,4},{4,68},{68,132},{132,196},{196,0... | collective-permute-start | bytes 1179656 | tf_op jit(solution)/shard_map/ppermute | solution.py:407
  29.8 19.3 %collective-permute-start.1 = (bf16[16,96,128]{2,1,0:T(8,128)(2,1)S(1)}, bf16[16,96,128]{2,1,0:T(8,128)(2,1)S(1)}, u32[]{:S(2)}, u32[]{:S(2)}) collective-permute-start(bf16[16,96,128]{2,1,0:T(8,128)(2,1)S(1)} %collective-permute-done), channel_id=1, source_target_pairs={{0,64},{64,128},{128,192},{192,4},{4,68},{68,132},{132,196},{196,0... | collective-permute-start | bytes 1179656 | tf_op jit(solution)/shard_map/ppermute | solution.py:407
  35.4 17.0 %collective-permute-start.5 = (bf16[16,96,128]{2,1,0:T(8,128)(2,1)S(1)}, bf16[16,96,128]{2,1,0:T(8,128)(2,1)S(1)}, u32[]{:S(2)}, u32[]{:S(2)}) collective-permute-start(bf16[16,96,128]{2,1,0:T(8,128)(2,1)S(1)} %collective-permute-done.3.refs_1_), channel_id=1, source_target_pairs={{0,64},{64,128},{128,192},{192,4},{4,68},{68,132},{132,196},{196,0... | collective-permute-start | bytes 1179656 | tf_op jit(solution)/shard_map/ppermute | solution.py:407
  49.1 7.8 %collective-permute-start.4 = (bf16[16,96,128]{2,1,0:T(8,128)(2,1)S(1)}, bf16[16,96,128]{2,1,0:T(8,128)(2,1)S(1)}, u32[]{:S(2)}, u32[]{:S(2)}) collective-permute-start(bf16[16,96,128]{2,1,0:T(8,128)(2,1)S(1)} %collective-permute-done.1.refs_1_), channel_id=1, source_target_pairs={{0,64},{64,128},{128,192},{192,4},{4,68},{68,132},{132,196},{196,0... | collective-permute-start | bytes 1179656 | tf_op jit(solution)/shard_map/ppermute | solution.py:407
  52.4 8.8 %collective-permute-start.7 = (bf16[16,96,128]{2,1,0:T(8,128)(2,1)S(1)}, bf16[16,96,128]{2,1,0:T(8,128)(2,1)S(1)}, u32[]{:S(2)}, u32[]{:S(2)}) collective-permute-start(bf16[16,96,128]{2,1,0:T(8,128)(2,1)S(1)} %collective-permute-done.5.refs_1_), channel_id=1, source_target_pairs={{0,64},{64,128},{128,192},{192,4},{4,68},{68,132},{132,196},{196,0... | collective-permute-start | bytes 1179656 | tf_op jit(solution)/shard_map/ppermute | solution.py:407
  57.0 8.4 %collective-permute-start.6 = (bf16[16,96,128]{2,1,0:T(8,128)(2,1)S(1)}, bf16[16,96,128]{2,1,0:T(8,128)(2,1)S(1)}, u32[]{:S(2)}, u32[]{:S(2)}) collective-permute-start(bf16[16,96,128]{2,1,0:T(8,128)(2,1)S(1)} %collective-permute-done.4.refs_1_), channel_id=1, source_target_pairs={{0,64},{64,128},{128,192},{192,4},{4,68},{68,132},{132,196},{196,0... | collective-permute-start | bytes 1179656 | tf_op jit(solution)/shard_map/ppermute | solution.py:407
  61.2 7.6 %collective-permute-start.8 = (bf16[16,96,128]{2,1,0:T(8,128)(2,1)S(1)}, bf16[16,96,128]{2,1,0:T(8,128)(2,1)S(1)}, u32[]{:S(2)}, u32[]{:S(2)}) collective-permute-start(bf16[16,96,128]{2,1,0:T(8,128)(2,1)S(1)} %collective-permute-done.7.refs_1_), channel_id=1, source_target_pairs={{0,64},{64,128},{128,192},{192,4},{4,68},{68,132},{132,196},{196,0... | collective-permute-start | bytes 1179656 | tf_op jit(solution)/shard_map/ppermute | solution.py:407
  68.8 34.0 %copy-start = (bf16[3,3,3,256,256]{4,3,2,1,0:T(8,128)(2,1)S(1)}, bf16[3,3,3,256,256]{4,3,2,1,0:T(8,128)(2,1)}, u32[]{:S(2)}) copy-start(bf16[3,3,3,256,256]{4,3,2,1,0:T(8,128)(2,1)} %w_out_ref.1) | copy-start | bytes 10616836
  68.9 34.0 %copy-start.1 = (bf16[3,3,3,16,256]{4,3,2,1,0:T(8,128)(2,1)S(1)}, bf16[3,3,3,16,256]{4,3,2,1,0:T(8,128)(2,1)}, u32[]{:S(2)}) copy-start(bf16[3,3,3,16,256]{4,3,2,1,0:T(8,128)(2,1)} %w_in_ref.1) | copy-start | bytes 663556
  68.9 34.0 %copy-start.2 = (f32[256]{0:T(256)S(1)}, f32[256]{0:T(256)}, u32[]{:S(2)}) copy-start(f32[256]{0:T(256)} %param.13) | copy-start | bytes 3076
  68.9 34.0 %copy-start.3 = (f32[256]{0:T(256)S(1)}, f32[256]{0:T(256)}, u32[]{:S(2)}) copy-start(f32[256]{0:T(256)} %param.15) | copy-start | bytes 3076
  70.1 3.3 %collective-permute-start.9 = (f32[80,1024]{1,0:T(8,128)S(1)}, f32[80,1024]{1,0:T(8,128)S(1)}, u32[]{:S(2)}, u32[]{:S(2)}) collective-permute-start(f32[80,1024]{1,0:T(8,128)S(1)} %bitcast.15), channel_id=1, source_target_pairs={{0,32},{32,0},{1,33},{33,1},{2,34},{34,2},{3,35},{35,3},{4,36},{36... | collective-permute-start | bytes 983048 | tf_op jit(solution)/shard_map/ppermute | solution.py:411
  99.0 3.9 %collective-permute-start.10 = (bf16[8,3,16,128]{3,2,1,0:T(8,128)(2,1)S(1)}, bf16[8,3,16,128]{3,2,1,0:T(8,128)(2,1)S(1)}, u32[]{:S(2)}, u32[]{:S(2)}) collective-permute-start(bf16[8,3,16,128]{3,2,1,0:T(8,128)(2,1)S(1)} %all_to_all.17.own_ref), channel_id=1, source_target_pairs={{0,32},{32,0},{1,33},{33,1},{2,34},{34,2},{3,35},{35,3},{4,36},{36... | collective-permute-start | bytes 294920 | tf_op jit(solution)/shard_map/ppermute | solution.py:411
where the time goes:
time: 108 us
  blocking collectives  44.4 us (41%)
  starting transfers between devices  31.8 us (29%)
  Pallas kernels  29.3 us (27%)
  waiting for transfers between devices  1.92 us (2%)
    all_to_all x3, blocking collectives, swapped(): return lax.all_to_all(value, axes, split_axis=0, concat_axis=0, tiled=True)  44.4 us
    ppermute x7, starting transfers between devices, hop(): return lax.ppermute(value, STACK, around())  24.5 us
    pallas_call x9, Pallas kernels, attend(): pl.pallas_call(functools.partial(attend_kernel, first), out_shape=jax.Sha...  21.4 us
    ppermute x4, starting transfers between devices, across(): return lax.ppermute(value, 'core', [(0, 1), (1, 0)])  7.24 us
    pallas_call x1, Pallas kernels, decode(): pl.pallas_call(decode_kernel, in_specs=[pl.BlockSpec(memory_space=pltpu.S...  4.94 us
    pallas_call x1, Pallas kernels, pack(): pl.pallas_call(pack_kernel, in_specs=[pl.BlockSpec(memory_space=pl.ANY)]...  2.34 us
  transfers between devices with their start and end apart: 11, of which 2 were waited for; matrix products, arithmetic and copies ran while one was open for 0% of the time, Pallas kernels for 19%

commit v1 on v0

--- a/solution.py
+++ b/solution.py
@@ -256,9 +256,9 @@
 
 
 def upsampled_conv(w_ref, act_ref, sum_ref):
-    def one(dt, _):
-        for p in range(2):
-            totals = [None, None]
+    for p in range(2):
+        totals = [None, None]
+        for dt in range(3):
             for i in range(2):
                 rows = []
                 for dx in range(3):
@@ -273,17 +273,13 @@
                             tap = tap + rows[dx]
                         blocks = []
                         for a in range(2):
-                            view = act_ref[a + p + i, pl.ds(dt, 2), q + j : q + j + 2]
+                            view = act_ref[a + p + i, dt : dt + 2, q + j : q + j + 2]
                             blocks.append(view.reshape(128, CH))
                         lhs = jnp.concatenate(blocks, axis=0)
                         part = jnp.dot(lhs, tap.astype(BF), preferred_element_type=F32)
                         totals[q] = part if totals[q] is None else totals[q] + part
-            for q in range(2):
-                sum_ref[2 * p + q] += totals[q]
-        return 0
-
-    sum_ref[...] = jnp.zeros(sum_ref.shape, F32)
-    lax.fori_loop(0, 3, one, 0)
+        for q in range(2):
+            sum_ref[2 * p + q] = totals[q]
 
 
 def decode_kernel(

time: 108 us -> 106 us (0.981); the launches traced: 108 us -> 104 us
  starting transfers between devices: 31.8 us -> 20.4 us
  Pallas kernels: 29.3 us -> 39.2 us
  blocking collectives: 44.4 us -> 40.8 us
  waiting for transfers between devices: 1.92 us -> 3.59 us
    ppermute x7, starting transfers between devices: 24.5 us -> 13.4 us  [hop(): return lax.ppermute(value, STACK, around())]
    pallas_call x9, Pallas kernels: 21.4 us -> 31.9 us  [attend(): pl.pallas_call(functools.partial(attend_kernel, first), out_shape=jax.Sha...]
    all_to_all x3, blocking collectives: 44.4 us -> 40.8 us  [swapped(): return lax.all_to_all(value, axes, split_axis=0, concat_axis=0, tiled=True)]
    ppermute x7, waiting for transfers between devices: 0.95 us -> 2.62 us  [hop(): return lax.ppermute(value, STACK, around())]
  transfers between devices with their start and end apart: 11 -> 11, of which waited for: 2 -> 5; matrix products, arithmetic and copies ran while one was open for 0% -> 0% of each run, Pallas kernels for 19% -> 29%
where the time goes in v1:
time: 106 us; the launch traced here: 104 us
  blocking collectives  40.8 us (38%)
  Pallas kernels  39.2 us (37%)
  starting transfers between devices  20.4 us (19%)
  waiting for transfers between devices  3.59 us (3%)
    all_to_all x3, blocking collectives, swapped(): return lax.all_to_all(value, axes, split_axis=0, concat_axis=0, tiled=True)  40.8 us
    pallas_call x9, Pallas kernels, attend(): pl.pallas_call(functools.partial(attend_kernel, first), out_shape=jax.Sha...  31.9 us
    ppermute x7, starting transfers between devices, hop(): return lax.ppermute(value, STACK, around())  13.4 us
    ppermute x4, starting transfers between devices, across(): return lax.ppermute(value, 'core', [(0, 1), (1, 0)])  7 us
    pallas_call x1, Pallas kernels, decode(): pl.pallas_call(decode_kernel, in_specs=[pl.BlockSpec(memory_space=pltpu.S...  4.29 us
    ppermute x7, waiting for transfers between devices, hop(): return lax.ppermute(value, STACK, around())  2.62 us
    pallas_call x1, Pallas kernels, pack(): pl.pallas_call(pack_kernel, in_specs=[pl.BlockSpec(memory_space=pl.ANY)]...  2.34 us
  transfers between devices with their start and end apart: 11, of which 5 were waited for; matrix products, arithmetic and copies ran while one was open for 0% of the time, Pallas kernels for 29%

profile of v1, /device:TPU:1, one launch (start us, length us, event | category | flops | bytes accessed | tf_op | source)
XLA Modules:
  0.0 104.3 jit_solution(848922756958061499)
XLA Ops:
  0.0 2.3 %pack.1 = bf16[16,160,128]{2,1,0:T(8,128)(2,1)} custom-call(bf16[64,2048]{1,0:T(8,128)(2,1)} %q_hbm.1, bf16[64,2048]{1,0:T(8,128)(2,1)} %k_hbm.1, bf16[64,2048]{1,0:T(8,128)(2,1)} %v_hbm.1, bf16[64,2048]{1,0:T(8,128)(2,1)} %bitcast.20), custom_call_target="tpu_custom_call" | custom-call | flops 16777216 | bytes 1048576 | tf_op jit(solution)/shard_map/pack/pallas_call | solution.py:64
  2.3 19.4 %all_to_all.15 = bf16[16,160,128]{2,1,0:T(8,128)(2,1)S(1)} all-to-all(bf16[16,160,128]{2,1,0:T(8,128)(2,1)} %pack.1), channel_id=1, replica_groups=mesh['zl'=4,'core'=2,'y'=4,'zh'=2,'x'=4] {'y','x'}, dimensions={0} | all-to-all | bytes 1310720 | tf_op jit(solution)/shard_map/all_to_all | solution.py:399
  21.8 2.2 %collective-permute-start = (bf16[16,96,128]{2,1,0:T(8,128)(2,1)S(1)}, bf16[16,96,128]{2,1,0:T(8,128)(2,1)S(1)}, u32[]{:S(2)}, u32[]{:S(2)}) collective-permute-start(bf16[16,96,128]{2,1,0:T(8,128)(2,1)S(1)} %slice.16.refs_1_), channel_id=1, source_target_pairs={{0,32},{32,0},{1,33},{33,1},{2,34},{34,2},{3,35},{35,3},{4,36},{36... | collective-permute-start | bytes 1179656 | tf_op jit(solution)/shard_map/ppermute | solution.py:407
  24.0 0.1 collective-permute-start.2
  24.1 5.7 %collective-permute-start.3 = (bf16[16,96,128]{2,1,0:T(8,128)(2,1)S(1)}, bf16[16,96,128]{2,1,0:T(8,128)(2,1)S(1)}, u32[]{:S(2)}, u32[]{:S(2)}) collective-permute-start(bf16[16,96,128]{2,1,0:T(8,128)(2,1)S(1)} %slice.16.refs_1_), channel_id=1, source_target_pairs={{0,64},{64,128},{128,192},{192,4},{4,68},{68,132},{132,196},{196,0... | collective-permute-start | bytes 1179656 | tf_op jit(solution)/shard_map/ppermute | solution.py:403
  29.7 0.1 pad_add_fusion.where_ref
  29.8 0.0 collective-permute-done
  29.8 1.1 %collective-permute-start.1 = (bf16[16,96,128]{2,1,0:T(8,128)(2,1)S(1)}, bf16[16,96,128]{2,1,0:T(8,128)(2,1)S(1)}, u32[]{:S(2)}, u32[]{:S(2)}) collective-permute-start(bf16[16,96,128]{2,1,0:T(8,128)(2,1)S(1)} %collective-permute-done), channel_id=1, source_target_pairs={{0,64},{64,128},{128,192},{192,4},{4,68},{68,132},{132,196},{196,0... | collective-permute-start | bytes 1179656 | tf_op jit(solution)/shard_map/ppermute | solution.py:403
  30.9 0.0 collective-permute-done.2
  30.9 0.1 pad_maximum_fusion.refs_0_
  30.9 15.0 %attend.9.refs_2_ = f32[2,80,1024]{2,1,0:T(8,128)S(1)} custom-call(bf16[2,1024,128]{2,1,0:T(8,128)(2,1)S(1)} %pad_maximum_fusion.refs_0_, bf16[16,96,128]{2,1,0:T(8,128)(2,1)S(1)} %slice.16.refs_1_), custom_call_target="tpu_custom_call" | custom-call | flops 1073741824 | bytes 2097152 | tf_op jit(solution)/shard_map/attend/pallas_call | solution.py:172
  45.9 0.0 collective-permute-done.3.refs_1_
  45.9 0.8 collective-permute-start.5
  46.7 2.4 %attend.10.refs_2_ = f32[2,80,1024]{2,1,0:T(8,128)S(1)} custom-call(bf16[2,1024,128]{2,1,0:T(8,128)(2,1)S(1)} %pad_maximum_fusion.refs_0_, bf16[16,96,128]{2,1,0:T(8,128)(2,1)S(1)} %collective-permute-done.3.refs_1_, f32[2,80,1024]{2,1,0:T(8,128)S(1)} %attend.9.refs_2_), custom_call_target="tpu_custom_call", output_to_operand_aliasing={{}: (2, {})} | custom-call | flops 1073741824 | bytes 2097152 | tf_op jit(solution)/shard_map/attend/pallas_call | solution.py:172
  49.1 0.0 collective-permute-done.1.refs_1_
  49.1 0.8 collective-permute-start.4
  49.9 2.4 %attend.11.refs_2_ = f32[2,80,1024]{2,1,0:T(8,128)S(1)} custom-call(bf16[2,1024,128]{2,1,0:T(8,128)(2,1)S(1)} %pad_maximum_fusion.refs_0_, bf16[16,96,128]{2,1,0:T(8,128)(2,1)S(1)} %collective-permute-done.1.refs_1_, f32[2,80,1024]{2,1,0:T(8,128)S(1)} %attend.10.refs_2_), custom_call_target="tpu_custom_call", output_to_operand_aliasing={{}: (2, {})} | custom-call | flops 1073741824 | bytes 2097152 | tf_op jit(solution)/shard_map/attend/pallas_call | solution.py:172
  52.4 0.5 collective-permute-done.5.refs_1_
  52.9 1.6 %collective-permute-start.7 = (bf16[16,96,128]{2,1,0:T(8,128)(2,1)S(1)}, bf16[16,96,128]{2,1,0:T(8,128)(2,1)S(1)}, u32[]{:S(2)}, u32[]{:S(2)}) collective-permute-start(bf16[16,96,128]{2,1,0:T(8,128)(2,1)S(1)} %collective-permute-done.5.refs_1_), channel_id=1, source_target_pairs={{0,64},{64,128},{128,192},{192,4},{4,68},{68,132},{132,196},{196,0... | collective-permute-start | bytes 1179656 | tf_op jit(solution)/shard_map/ppermute | solution.py:403
  54.5 2.4 %attend.12.refs_2_ = f32[2,80,1024]{2,1,0:T(8,128)S(1)} custom-call(bf16[2,1024,128]{2,1,0:T(8,128)(2,1)S(1)} %pad_maximum_fusion.refs_0_, bf16[16,96,128]{2,1,0:T(8,128)(2,1)S(1)} %collective-permute-done.5.refs_1_, f32[2,80,1024]{2,1,0:T(8,128)S(1)} %attend.11.refs_2_), custom_call_target="tpu_custom_call", output_to_operand_aliasing={{}: (2, {})} | custom-call | flops 1073741824 | bytes 2097152 | tf_op jit(solution)/shard_map/attend/pallas_call | solution.py:172
  57.0 0.0 collective-permute-done.4.refs_1_
  57.0 1.8 %collective-permute-start.6 = (bf16[16,96,128]{2,1,0:T(8,128)(2,1)S(1)}, bf16[16,96,128]{2,1,0:T(8,128)(2,1)S(1)}, u32[]{:S(2)}, u32[]{:S(2)}) collective-permute-start(bf16[16,96,128]{2,1,0:T(8,128)(2,1)S(1)} %collective-permute-done.4.refs_1_), channel_id=1, source_target_pairs={{0,64},{64,128},{128,192},{192,4},{4,68},{68,132},{132,196},{196,0... | collective-permute-start | bytes 1179656 | tf_op jit(solution)/shard_map/ppermute | solution.py:403
  58.8 2.4 %attend.13.refs_2_ = f32[2,80,1024]{2,1,0:T(8,128)S(1)} custom-call(bf16[2,1024,128]{2,1,0:T(8,128)(2,1)S(1)} %pad_maximum_fusion.refs_0_, bf16[16,96,128]{2,1,0:T(8,128)(2,1)S(1)} %collective-permute-done.4.refs_1_, f32[2,80,1024]{2,1,0:T(8,128)S(1)} %attend.12.refs_2_), custom_call_target="tpu_custom_call", output_to_operand_aliasing={{}: (2, {})} | custom-call | flops 1073741824 | bytes 2097152 | tf_op jit(solution)/shard_map/attend/pallas_call | solution.py:172
  61.2 0.1 collective-permute-done.7.refs_1_
  61.3 1.6 %collective-permute-start.8 = (bf16[16,96,128]{2,1,0:T(8,128)(2,1)S(1)}, bf16[16,96,128]{2,1,0:T(8,128)(2,1)S(1)}, u32[]{:S(2)}, u32[]{:S(2)}) collective-permute-start(bf16[16,96,128]{2,1,0:T(8,128)(2,1)S(1)} %collective-permute-done.7.refs_1_), channel_id=1, source_target_pairs={{0,64},{64,128},{128,192},{192,4},{4,68},{68,132},{132,196},{196,0... | collective-permute-start | bytes 1179656 | tf_op jit(solution)/shard_map/ppermute | solution.py:403
  63.0 2.4 %attend.14.refs_2_ = f32[2,80,1024]{2,1,0:T(8,128)S(1)} custom-call(bf16[2,1024,128]{2,1,0:T(8,128)(2,1)S(1)} %pad_maximum_fusion.refs_0_, bf16[16,96,128]{2,1,0:T(8,128)(2,1)S(1)} %collective-permute-done.7.refs_1_, f32[2,80,1024]{2,1,0:T(8,128)S(1)} %attend.13.refs_2_), custom_call_target="tpu_custom_call", output_to_operand_aliasing={{}: (2, {})} | custom-call | flops 1073741824 | bytes 2097152 | tf_op jit(solution)/shard_map/attend/pallas_call | solution.py:172
  65.4 0.1 collective-permute-done.6.refs_1_
  65.5 2.4 %attend.15 = f32[2,80,1024]{2,1,0:T(8,128)S(1)} custom-call(bf16[2,1024,128]{2,1,0:T(8,128)(2,1)S(1)} %pad_maximum_fusion.refs_0_, bf16[16,96,128]{2,1,0:T(8,128)(2,1)S(1)} %collective-permute-done.6.refs_1_, f32[2,80,1024]{2,1,0:T(8,128)S(1)} %attend.14.refs_2_), custom_call_target="tpu_custom_call", output_to_operand_aliasing={{}: (2, {})} | custom-call | flops 1073741824 | bytes 2097152 | tf_op jit(solution)/shard_map/attend/pallas_call | solution.py:172
  68.0 1.8 %collective-permute-done.8.refs_1_ = bf16[16,96,128]{2,1,0:T(8,128)(2,1)S(1)} collective-permute-done((bf16[16,96,128]{2,1,0:T(8,128)(2,1)S(1)}, bf16[16,96,128]{2,1,0:T(8,128)(2,1)S(1)}, u32[]{:S(2)}, u32[]{:S(2)}) %collective-permute-start.8) | collective-permute-done | bytes 393248 | tf_op jit(solution)/shard_map/ppermute | solution.py:403
  69.8 0.1 fusion
  69.8 0.0 copy-start
  69.8 0.0 copy-start.1
  69.8 0.0 copy-start.2
  69.9 0.0 copy-start.3
  69.9 1.2 %attend.16 = f32[1,80,1024]{2,1,0:T(8,128)S(1)} custom-call(bf16[1,1024,128]{2,1,0:T(8,128)(2,1)S(1)} %bitcast.17, bf16[16,96,128]{2,1,0:T(8,128)(2,1)S(1)} %collective-permute-done.8.refs_1_, f32[1,80,1024]{2,1,0:T(8,128)S(1)} %get-tuple-element.52.refs_2_), custom_call_target="tpu_custom_call", output_to_operand_aliasing={{}: (2, {})} | custom-call | flops 536870912 | bytes 1048576 | tf_op jit(solution)/shard_map/attend/pallas_call | solution.py:172
  71.1 1.9 %collective-permute-start.9 = (f32[80,1024]{1,0:T(8,128)S(1)}, f32[80,1024]{1,0:T(8,128)S(1)}, u32[]{:S(2)}, u32[]{:S(2)}) collective-permute-start(f32[80,1024]{1,0:T(8,128)S(1)} %bitcast.15), channel_id=1, source_target_pairs={{0,32},{32,0},{1,33},{33,1},{2,34},{34,2},{3,35},{35,3},{4,36},{36... | collective-permute-start | bytes 983048 | tf_op jit(solution)/shard_map/ppermute | solution.py:407
  73.1 1.2 %attend.17 = f32[1,80,1024]{2,1,0:T(8,128)S(1)} custom-call(bf16[1,1024,128]{2,1,0:T(8,128)(2,1)S(1)} %bitcast.14, bf16[16,96,128]{2,1,0:T(8,128)(2,1)S(1)} %collective-permute-done.8.refs_1_, f32[1,80,1024]{2,1,0:T(8,128)S(1)} %get-tuple-element.49.refs_2_), custom_call_target="tpu_custom_call", output_to_operand_aliasing={{}: (2, {})} | custom-call | flops 536870912 | bytes 1048576 | tf_op jit(solution)/shard_map/attend/pallas_call | solution.py:172
  74.3 0.0 collective-permute-done.9.other_ref
  74.3 0.5 join.1
  74.8 12.3 %all_to_all.16.in_ref = bf16[16,3,32,128]{3,2,1,0:T(8,128)(2,1)S(1)} all-to-all(bf16[16,3,32,128]{3,2,1,0:T(8,128)(2,1)S(1)} %join.1), channel_id=1, replica_groups=mesh['zl'=4,'core'=2,'y'=4,'zh'=2,'x'=4] {'y','x'}, dimensions={0} | all-to-all | bytes 786432 | tf_op jit(solution)/shard_map/all_to_all | solution.py:399
  87.1 0.1 patch_sum.1
  87.3 9.0 %all_to_all.17.own_ref = bf16[8,3,16,128]{3,2,1,0:T(8,128)(2,1)S(1)} all-to-all(bf16[8,3,16,128]{3,2,1,0:T(8,128)(2,1)S(1)} %patch_sum.1), channel_id=1, replica_groups=mesh['zl'=4,'core'=2,'y'=4,'zh'=2,'x'=4] {'zl','zh'}, dimensions={0} | all-to-all | bytes 196608 | tf_op jit(solution)/shard_map/all_to_all | solution.py:399
  96.3 2.8 %collective-permute-start.10 = (bf16[8,3,16,128]{3,2,1,0:T(8,128)(2,1)S(1)}, bf16[8,3,16,128]{3,2,1,0:T(8,128)(2,1)S(1)}, u32[]{:S(2)}, u32[]{:S(2)}) collective-permute-start(bf16[8,3,16,128]{3,2,1,0:T(8,128)(2,1)S(1)} %all_to_all.17.own_ref), channel_id=1, source_target_pairs={{0,32},{32,0},{1,33},{33,1},{2,34},{34,2},{3,35},{35,3},{4,36},{36... | collective-permute-start | bytes 294920 | tf_op jit(solution)/shard_map/ppermute | solution.py:407
  99.1 0.9 collective-permute-done.10.other_ref
  100.0 0.0 copy-done
  100.0 0.0 copy-done.1
  100.0 0.0 copy-done.2
  100.0 4.3 %decode.1 = bf16[2,32,4,4,256]{4,3,2,1,0:T(4,128)(2,1)} custom-call(s32[2]{0:T(128)S(1)} %pad_add_fusion.where_ref, bf16[8,3,16,128]{3,2,1,0:T(8,128)(2,1)S(1)} %all_to_all.17.own_ref, bf16[8,3,16,128]{3,2,1,0:T(8,128)(2,1)S(1)} %collective-permute-done.10.other_ref, bf16[3,3,3,16,256]{4,3,2,1,0:T(8,128)(2,1)S(1)} %copy-done.1, f32[1,256]{1,0:T(1,128)S(1)} %bitcast.18, ...), custom_call_target="tpu_custom_call" | custom-call | flops 2147483648 | bytes 10485760 | tf_op jit(solution)/shard_map/decode/pallas_call | solution.py:373
  (3 shorter events, 0.0 us)
Async XLA Ops:
  21.8 8.0 %collective-permute-start = (bf16[16,96,128]{2,1,0:T(8,128)(2,1)S(1)}, bf16[16,96,128]{2,1,0:T(8,128)(2,1)S(1)}, u32[]{:S(2)}, u32[]{:S(2)}) collective-permute-start(bf16[16,96,128]{2,1,0:T(8,128)(2,1)S(1)} %slice.16.refs_1_), channel_id=1, source_target_pairs={{0,32},{32,0},{1,33},{33,1},{2,34},{34,2},{3,35},{35,3},{4,36},{36... | collective-permute-start | bytes 1179656 | tf_op jit(solution)/shard_map/ppermute | solution.py:407
  24.0 6.9 %collective-permute-start.2 = (bf16[1024,128]{1,0:T(8,128)(2,1)S(1)}, bf16[1024,128]{1,0:T(8,128)(2,1)S(1)}, u32[]{:S(2)}, u32[]{:S(2)}) collective-permute-start(bf16[1024,128]{1,0:T(8,128)(2,1)S(1)} %bitcast.12), channel_id=1, source_target_pairs={{0,32},{32,0},{1,33},{33,1},{2,34},{34,2},{3,35},{35,3},{4,36},{36... | collective-permute-start | bytes 786440 | tf_op jit(solution)/shard_map/ppermute | solution.py:407
  24.1 21.8 %collective-permute-start.3 = (bf16[16,96,128]{2,1,0:T(8,128)(2,1)S(1)}, bf16[16,96,128]{2,1,0:T(8,128)(2,1)S(1)}, u32[]{:S(2)}, u32[]{:S(2)}) collective-permute-start(bf16[16,96,128]{2,1,0:T(8,128)(2,1)S(1)} %slice.16.refs_1_), channel_id=1, source_target_pairs={{0,64},{64,128},{128,192},{192,4},{4,68},{68,132},{132,196},{196,0... | collective-permute-start | bytes 1179656 | tf_op jit(solution)/shard_map/ppermute | solution.py:403
  29.8 19.3 %collective-permute-start.1 = (bf16[16,96,128]{2,1,0:T(8,128)(2,1)S(1)}, bf16[16,96,128]{2,1,0:T(8,128)(2,1)S(1)}, u32[]{:S(2)}, u32[]{:S(2)}) collective-permute-start(bf16[16,96,128]{2,1,0:T(8,128)(2,1)S(1)} %collective-permute-done), channel_id=1, source_target_pairs={{0,64},{64,128},{128,192},{192,4},{4,68},{68,132},{132,196},{196,0... | collective-permute-start | bytes 1179656 | tf_op jit(solution)/shard_map/ppermute | solution.py:403
  45.9 7.0 %collective-permute-start.5 = (bf16[16,96,128]{2,1,0:T(8,128)(2,1)S(1)}, bf16[16,96,128]{2,1,0:T(8,128)(2,1)S(1)}, u32[]{:S(2)}, u32[]{:S(2)}) collective-permute-start(bf16[16,96,128]{2,1,0:T(8,128)(2,1)S(1)} %collective-permute-done.3.refs_1_), channel_id=1, source_target_pairs={{0,64},{64,128},{128,192},{192,4},{4,68},{68,132},{132,196},{196,0... | collective-permute-start | bytes 1179656 | tf_op jit(solution)/shard_map/ppermute | solution.py:403
  49.1 7.8 %collective-permute-start.4 = (bf16[16,96,128]{2,1,0:T(8,128)(2,1)S(1)}, bf16[16,96,128]{2,1,0:T(8,128)(2,1)S(1)}, u32[]{:S(2)}, u32[]{:S(2)}) collective-permute-start(bf16[16,96,128]{2,1,0:T(8,128)(2,1)S(1)} %collective-permute-done.1.refs_1_), channel_id=1, source_target_pairs={{0,64},{64,128},{128,192},{192,4},{4,68},{68,132},{132,196},{196,0... | collective-permute-start | bytes 1179656 | tf_op jit(solution)/shard_map/ppermute | solution.py:403
  52.9 8.4 %collective-permute-start.7 = (bf16[16,96,128]{2,1,0:T(8,128)(2,1)S(1)}, bf16[16,96,128]{2,1,0:T(8,128)(2,1)S(1)}, u32[]{:S(2)}, u32[]{:S(2)}) collective-permute-start(bf16[16,96,128]{2,1,0:T(8,128)(2,1)S(1)} %collective-permute-done.5.refs_1_), channel_id=1, source_target_pairs={{0,64},{64,128},{128,192},{192,4},{4,68},{68,132},{132,196},{196,0... | collective-permute-start | bytes 1179656 | tf_op jit(solution)/shard_map/ppermute | solution.py:403
  57.0 8.6 %collective-permute-start.6 = (bf16[16,96,128]{2,1,0:T(8,128)(2,1)S(1)}, bf16[16,96,128]{2,1,0:T(8,128)(2,1)S(1)}, u32[]{:S(2)}, u32[]{:S(2)}) collective-permute-start(bf16[16,96,128]{2,1,0:T(8,128)(2,1)S(1)} %collective-permute-done.4.refs_1_), channel_id=1, source_target_pairs={{0,64},{64,128},{128,192},{192,4},{4,68},{68,132},{132,196},{196,0... | collective-permute-start | bytes 1179656 | tf_op jit(solution)/shard_map/ppermute | solution.py:403
  61.3 8.4 %collective-permute-start.8 = (bf16[16,96,128]{2,1,0:T(8,128)(2,1)S(1)}, bf16[16,96,128]{2,1,0:T(8,128)(2,1)S(1)}, u32[]{:S(2)}, u32[]{:S(2)}) collective-permute-start(bf16[16,96,128]{2,1,0:T(8,128)(2,1)S(1)} %collective-permute-done.7.refs_1_), channel_id=1, source_target_pairs={{0,64},{64,128},{128,192},{192,4},{4,68},{68,132},{132,196},{196,0... | collective-permute-start | bytes 1179656 | tf_op jit(solution)/shard_map/ppermute | solution.py:403
  69.8 30.2 %copy-start = (bf16[3,3,3,256,256]{4,3,2,1,0:T(8,128)(2,1)S(1)}, bf16[3,3,3,256,256]{4,3,2,1,0:T(8,128)(2,1)}, u32[]{:S(2)}) copy-start(bf16[3,3,3,256,256]{4,3,2,1,0:T(8,128)(2,1)} %w_out_ref.1) | copy-start | bytes 10616836
  69.8 30.2 %copy-start.1 = (bf16[3,3,3,16,256]{4,3,2,1,0:T(8,128)(2,1)S(1)}, bf16[3,3,3,16,256]{4,3,2,1,0:T(8,128)(2,1)}, u32[]{:S(2)}) copy-start(bf16[3,3,3,16,256]{4,3,2,1,0:T(8,128)(2,1)} %w_in_ref.1) | copy-start | bytes 663556
  69.8 30.2 %copy-start.2 = (f32[256]{0:T(256)S(1)}, f32[256]{0:T(256)}, u32[]{:S(2)}) copy-start(f32[256]{0:T(256)} %param.13) | copy-start | bytes 3076
  69.9 30.2 %copy-start.3 = (f32[256]{0:T(256)S(1)}, f32[256]{0:T(256)}, u32[]{:S(2)}) copy-start(f32[256]{0:T(256)} %param.15) | copy-start | bytes 3076
  71.1 3.2 %collective-permute-start.9 = (f32[80,1024]{1,0:T(8,128)S(1)}, f32[80,1024]{1,0:T(8,128)S(1)}, u32[]{:S(2)}, u32[]{:S(2)}) collective-permute-start(f32[80,1024]{1,0:T(8,128)S(1)} %bitcast.15), channel_id=1, source_target_pairs={{0,32},{32,0},{1,33},{33,1},{2,34},{34,2},{3,35},{35,3},{4,36},{36... | collective-permute-start | bytes 983048 | tf_op jit(solution)/shard_map/ppermute | solution.py:407
  96.3 3.7 %collective-permute-start.10 = (bf16[8,3,16,128]{3,2,1,0:T(8,128)(2,1)S(1)}, bf16[8,3,16,128]{3,2,1,0:T(8,128)(2,1)S(1)}, u32[]{:S(2)}, u32[]{:S(2)}) collective-permute-start(bf16[8,3,16,128]{3,2,1,0:T(8,128)(2,1)S(1)} %all_to_all.17.own_ref), channel_id=1, source_target_pairs={{0,32},{32,0},{1,33},{33,1},{2,34},{34,2},{3,35},{35,3},{4,36},{36... | collective-permute-start | bytes 294920 | tf_op jit(solution)/shard_map/ppermute | solution.py:407

commit v2 on v1

--- a/solution.py
+++ b/solution.py
@@ -388,7 +388,7 @@
 
 def around():
     pairs = []
-    for core, step in ((0, 1), (1, -1)):
+    for core, step in ((0, -1), (1, 1)):
         for z in range(8):
             to = (z + step) % 8
             pairs.append(((z % 4) * 4 + core * 2 + z // 4, (to % 4) * 4 + core * 2 + to // 4))

time: 106 us -> 106 us (level); the launches traced: 104 us -> 106 us
  waiting for transfers between devices: 3.59 us -> 21.9 us
  Pallas kernels: 39.2 us -> 28.6 us
  starting transfers between devices: 20.4 us -> 12.5 us
  blocking collectives: 40.8 us -> 42.5 us
    ppermute x7, waiting for transfers between devices: 2.62 us -> 20.9 us  [hop(): return lax.ppermute(value, STACK, around())]
    pallas_call x9, Pallas kernels: 31.9 us -> 21.4 us  [attend(): pl.pallas_call(functools.partial(attend_kernel, first), out_shape=jax.Sha...]
    ppermute x7, starting transfers between devices: 13.4 us -> 4.24 us  [hop(): return lax.ppermute(value, STACK, around())]
    all_to_all x3, blocking collectives: 40.8 us -> 42.5 us  [swapped(): return lax.all_to_all(value, axes, split_axis=0, concat_axis=0, tiled=True)]
    ppermute x4, starting transfers between devices: 7 us -> 8.24 us  [across(): return lax.ppermute(value, 'core', [(0, 1), (1, 0)])]
  transfers between devices with their start and end apart: 11 -> 11, of which waited for: 5 -> 8; matrix products, arithmetic and copies ran while one was open for 0% -> 0% of each run, Pallas kernels for 29% -> 19%
where the time goes in v2:
time: 106 us
  blocking collectives  42.5 us (40%)
  Pallas kernels  28.6 us (27%)
  waiting for transfers between devices  21.9 us (21%)
  starting transfers between devices  12.5 us (12%)
    all_to_all x3, blocking collectives, swapped(): return lax.all_to_all(value, axes, split_axis=0, concat_axis=0, tiled=True)  42.5 us
    pallas_call x9, Pallas kernels, attend(): pl.pallas_call(functools.partial(attend_kernel, first), out_shape=jax.Sha...  21.4 us
    ppermute x7, waiting for transfers between devices, hop(): return lax.ppermute(value, STACK, around())  20.9 us
    ppermute x4, starting transfers between devices, across(): return lax.ppermute(value, 'core', [(0, 1), (1, 0)])  8.24 us
    pallas_call x1, Pallas kernels, decode(): pl.pallas_call(decode_kernel, in_specs=[pl.BlockSpec(memory_space=pltpu.S...  4.29 us
    ppermute x7, starting transfers between devices, hop(): return lax.ppermute(value, STACK, around())  4.24 us
    pallas_call x1, Pallas kernels, pack(): pl.pallas_call(pack_kernel, in_specs=[pl.BlockSpec(memory_space=pl.ANY)]...  2.34 us
  transfers between devices with their start and end apart: 11, of which 8 were waited for; matrix products, arithmetic and copies ran while one was open for 0% of the time, Pallas kernels for 19%

profile of v2, /device:TPU:1, one launch (start us, length us, event | category | flops | bytes accessed | tf_op | source)
XLA Modules:
  0.0 105.9 jit_solution(1311996260394893890)
XLA Ops:
  0.0 2.3 %pack.1 = bf16[16,160,128]{2,1,0:T(8,128)(2,1)} custom-call(bf16[64,2048]{1,0:T(8,128)(2,1)} %q_hbm.1, bf16[64,2048]{1,0:T(8,128)(2,1)} %k_hbm.1, bf16[64,2048]{1,0:T(8,128)(2,1)} %v_hbm.1, bf16[64,2048]{1,0:T(8,128)(2,1)} %bitcast.20), custom_call_target="tpu_custom_call" | custom-call | flops 16777216 | bytes 1048576 | tf_op jit(solution)/shard_map/pack/pallas_call | solution.py:64
  2.3 19.4 %all_to_all.15 = bf16[16,160,128]{2,1,0:T(8,128)(2,1)S(1)} all-to-all(bf16[16,160,128]{2,1,0:T(8,128)(2,1)} %pack.1), channel_id=1, replica_groups=mesh['zl'=4,'core'=2,'y'=4,'zh'=2,'x'=4] {'y','x'}, dimensions={0} | all-to-all | bytes 1310720 | tf_op jit(solution)/shard_map/all_to_all | solution.py:399
  21.8 2.2 %collective-permute-start = (bf16[16,96,128]{2,1,0:T(8,128)(2,1)S(1)}, bf16[16,96,128]{2,1,0:T(8,128)(2,1)S(1)}, u32[]{:S(2)}, u32[]{:S(2)}) collective-permute-start(bf16[16,96,128]{2,1,0:T(8,128)(2,1)S(1)} %slice.16.refs_1_), channel_id=1, source_target_pairs={{0,32},{32,0},{1,33},{33,1},{2,34},{34,2},{3,35},{35,3},{4,36},{36... | collective-permute-start | bytes 1179656 | tf_op jit(solution)/shard_map/ppermute | solution.py:407
  24.0 0.1 collective-permute-start.2
  24.1 1.7 %collective-permute-start.3 = (bf16[16,96,128]{2,1,0:T(8,128)(2,1)S(1)}, bf16[16,96,128]{2,1,0:T(8,128)(2,1)S(1)}, u32[]{:S(2)}, u32[]{:S(2)}) collective-permute-start(bf16[16,96,128]{2,1,0:T(8,128)(2,1)S(1)} %slice.16.refs_1_), channel_id=1, source_target_pairs={{0,196},{64,0},{128,64},{192,128},{4,192},{68,4},{132,68},{196,132... | collective-permute-start | bytes 1179656 | tf_op jit(solution)/shard_map/ppermute | solution.py:403
  25.8 0.1 pad_add_fusion.where_ref
  25.9 0.0 collective-permute-done
  25.9 1.6 %collective-permute-start.1 = (bf16[16,96,128]{2,1,0:T(8,128)(2,1)S(1)}, bf16[16,96,128]{2,1,0:T(8,128)(2,1)S(1)}, u32[]{:S(2)}, u32[]{:S(2)}) collective-permute-start(bf16[16,96,128]{2,1,0:T(8,128)(2,1)S(1)} %collective-permute-done), channel_id=1, source_target_pairs={{0,196},{64,0},{128,64},{192,128},{4,192},{68,4},{132,68},{196,132... | collective-permute-start | bytes 1179656 | tf_op jit(solution)/shard_map/ppermute | solution.py:403
  27.5 0.0 collective-permute-done.2
  27.5 0.1 pad_maximum_fusion.refs_0_
  27.6 4.4 %attend.9.refs_2_ = f32[2,80,1024]{2,1,0:T(8,128)S(1)} custom-call(bf16[2,1024,128]{2,1,0:T(8,128)(2,1)S(1)} %pad_maximum_fusion.refs_0_, bf16[16,96,128]{2,1,0:T(8,128)(2,1)S(1)} %slice.16.refs_1_), custom_call_target="tpu_custom_call" | custom-call | flops 1073741824 | bytes 2097152 | tf_op jit(solution)/shard_map/attend/pallas_call | solution.py:172
  32.0 2.9 %collective-permute-done.3.refs_1_ = bf16[16,96,128]{2,1,0:T(8,128)(2,1)S(1)} collective-permute-done((bf16[16,96,128]{2,1,0:T(8,128)(2,1)S(1)}, bf16[16,96,128]{2,1,0:T(8,128)(2,1)S(1)}, u32[]{:S(2)}, u32[]{:S(2)}) %collective-permute-start.3) | collective-permute-done | bytes 393248 | tf_op jit(solution)/shard_map/ppermute | solution.py:403
  34.9 0.0 collective-permute-start.5
  34.9 2.4 %attend.10.refs_2_ = f32[2,80,1024]{2,1,0:T(8,128)S(1)} custom-call(bf16[2,1024,128]{2,1,0:T(8,128)(2,1)S(1)} %pad_maximum_fusion.refs_0_, bf16[16,96,128]{2,1,0:T(8,128)(2,1)S(1)} %collective-permute-done.3.refs_1_, f32[2,80,1024]{2,1,0:T(8,128)S(1)} %attend.9.refs_2_), custom_call_target="tpu_custom_call", output_to_operand_aliasing={{}: (2, {})} | custom-call | flops 1073741824 | bytes 2097152 | tf_op jit(solution)/shard_map/attend/pallas_call | solution.py:172
  37.3 1.8 %collective-permute-done.1.refs_1_ = bf16[16,96,128]{2,1,0:T(8,128)(2,1)S(1)} collective-permute-done((bf16[16,96,128]{2,1,0:T(8,128)(2,1)S(1)}, bf16[16,96,128]{2,1,0:T(8,128)(2,1)S(1)}, u32[]{:S(2)}, u32[]{:S(2)}) %collective-permute-start.1) | collective-permute-done | bytes 393248 | tf_op jit(solution)/shard_map/ppermute | solution.py:403
  39.1 0.0 collective-permute-start.4
  39.1 2.4 %attend.11.refs_2_ = f32[2,80,1024]{2,1,0:T(8,128)S(1)} custom-call(bf16[2,1024,128]{2,1,0:T(8,128)(2,1)S(1)} %pad_maximum_fusion.refs_0_, bf16[16,96,128]{2,1,0:T(8,128)(2,1)S(1)} %collective-permute-done.1.refs_1_, f32[2,80,1024]{2,1,0:T(8,128)S(1)} %attend.10.refs_2_), custom_call_target="tpu_custom_call", output_to_operand_aliasing={{}: (2, {})} | custom-call | flops 1073741824 | bytes 2097152 | tf_op jit(solution)/shard_map/attend/pallas_call | solution.py:172
  41.5 10.0 %collective-permute-done.5.refs_1_ = bf16[16,96,128]{2,1,0:T(8,128)(2,1)S(1)} collective-permute-done((bf16[16,96,128]{2,1,0:T(8,128)(2,1)S(1)}, bf16[16,96,128]{2,1,0:T(8,128)(2,1)S(1)}, u32[]{:S(2)}, u32[]{:S(2)}) %collective-permute-start.5) | collective-permute-done | bytes 393248 | tf_op jit(solution)/shard_map/ppermute | solution.py:403
  51.5 0.0 collective-permute-start.7
  51.5 2.4 %attend.12.refs_2_ = f32[2,80,1024]{2,1,0:T(8,128)S(1)} custom-call(bf16[2,1024,128]{2,1,0:T(8,128)(2,1)S(1)} %pad_maximum_fusion.refs_0_, bf16[16,96,128]{2,1,0:T(8,128)(2,1)S(1)} %collective-permute-done.5.refs_1_, f32[2,80,1024]{2,1,0:T(8,128)S(1)} %attend.11.refs_2_), custom_call_target="tpu_custom_call", output_to_operand_aliasing={{}: (2, {})} | custom-call | flops 1073741824 | bytes 2097152 | tf_op jit(solution)/shard_map/attend/pallas_call | solution.py:172
  54.0 1.8 %collective-permute-done.4.refs_1_ = bf16[16,96,128]{2,1,0:T(8,128)(2,1)S(1)} collective-permute-done((bf16[16,96,128]{2,1,0:T(8,128)(2,1)S(1)}, bf16[16,96,128]{2,1,0:T(8,128)(2,1)S(1)}, u32[]{:S(2)}, u32[]{:S(2)}) %collective-permute-start.4) | collective-permute-done | bytes 393248 | tf_op jit(solution)/shard_map/ppermute | solution.py:403
  55.7 0.9 collective-permute-start.6
  56.6 2.4 %attend.13.refs_2_ = f32[2,80,1024]{2,1,0:T(8,128)S(1)} custom-call(bf16[2,1024,128]{2,1,0:T(8,128)(2,1)S(1)} %pad_maximum_fusion.refs_0_, bf16[16,96,128]{2,1,0:T(8,128)(2,1)S(1)} %collective-permute-done.4.refs_1_, f32[2,80,1024]{2,1,0:T(8,128)S(1)} %attend.12.refs_2_), custom_call_target="tpu_custom_call", output_to_operand_aliasing={{}: (2, {})} | custom-call | flops 1073741824 | bytes 2097152 | tf_op jit(solution)/shard_map/attend/pallas_call | solution.py:172
  59.0 0.9 collective-permute-done.7.refs_1_
  59.9 0.0 collective-permute-start.8
  60.0 2.4 %attend.14.refs_2_ = f32[2,80,1024]{2,1,0:T(8,128)S(1)} custom-call(bf16[2,1024,128]{2,1,0:T(8,128)(2,1)S(1)} %pad_maximum_fusion.refs_0_, bf16[16,96,128]{2,1,0:T(8,128)(2,1)S(1)} %collective-permute-done.7.refs_1_, f32[2,80,1024]{2,1,0:T(8,128)S(1)} %attend.13.refs_2_), custom_call_target="tpu_custom_call", output_to_operand_aliasing={{}: (2, {})} | custom-call | flops 1073741824 | bytes 2097152 | tf_op jit(solution)/shard_map/attend/pallas_call | solution.py:172
  62.4 1.8 %collective-permute-done.6.refs_1_ = bf16[16,96,128]{2,1,0:T(8,128)(2,1)S(1)} collective-permute-done((bf16[16,96,128]{2,1,0:T(8,128)(2,1)S(1)}, bf16[16,96,128]{2,1,0:T(8,128)(2,1)S(1)}, u32[]{:S(2)}, u32[]{:S(2)}) %collective-permute-start.6) | collective-permute-done | bytes 393248 | tf_op jit(solution)/shard_map/ppermute | solution.py:403
  64.2 2.4 %attend.15 = f32[2,80,1024]{2,1,0:T(8,128)S(1)} custom-call(bf16[2,1024,128]{2,1,0:T(8,128)(2,1)S(1)} %pad_maximum_fusion.refs_0_, bf16[16,96,128]{2,1,0:T(8,128)(2,1)S(1)} %collective-permute-done.6.refs_1_, f32[2,80,1024]{2,1,0:T(8,128)S(1)} %attend.14.refs_2_), custom_call_target="tpu_custom_call", output_to_operand_aliasing={{}: (2, {})} | custom-call | flops 1073741824 | bytes 2097152 | tf_op jit(solution)/shard_map/attend/pallas_call | solution.py:172
  66.6 1.8 %collective-permute-done.8.refs_1_ = bf16[16,96,128]{2,1,0:T(8,128)(2,1)S(1)} collective-permute-done((bf16[16,96,128]{2,1,0:T(8,128)(2,1)S(1)}, bf16[16,96,128]{2,1,0:T(8,128)(2,1)S(1)}, u32[]{:S(2)}, u32[]{:S(2)}) %collective-permute-start.8) | collective-permute-done | bytes 393248 | tf_op jit(solution)/shard_map/ppermute | solution.py:403
  68.4 0.1 fusion
  68.4 0.0 copy-start
  68.4 0.0 copy-start.1
  68.5 0.0 copy-start.2
  68.5 0.0 copy-start.3
  68.5 1.2 %attend.16 = f32[1,80,1024]{2,1,0:T(8,128)S(1)} custom-call(bf16[1,1024,128]{2,1,0:T(8,128)(2,1)S(1)} %bitcast.17, bf16[16,96,128]{2,1,0:T(8,128)(2,1)S(1)} %collective-permute-done.8.refs_1_, f32[1,80,1024]{2,1,0:T(8,128)S(1)} %get-tuple-element.52.refs_2_), custom_call_target="tpu_custom_call", output_to_operand_aliasing={{}: (2, {})} | custom-call | flops 536870912 | bytes 1048576 | tf_op jit(solution)/shard_map/attend/pallas_call | solution.py:172
  69.7 3.0 %collective-permute-start.9 = (f32[80,1024]{1,0:T(8,128)S(1)}, f32[80,1024]{1,0:T(8,128)S(1)}, u32[]{:S(2)}, u32[]{:S(2)}) collective-permute-start(f32[80,1024]{1,0:T(8,128)S(1)} %bitcast.15), channel_id=1, source_target_pairs={{0,32},{32,0},{1,33},{33,1},{2,34},{34,2},{3,35},{35,3},{4,36},{36... | collective-permute-start | bytes 983048 | tf_op jit(solution)/shard_map/ppermute | solution.py:407
  72.7 1.2 %attend.17 = f32[1,80,1024]{2,1,0:T(8,128)S(1)} custom-call(bf16[1,1024,128]{2,1,0:T(8,128)(2,1)S(1)} %bitcast.14, bf16[16,96,128]{2,1,0:T(8,128)(2,1)S(1)} %collective-permute-done.8.refs_1_, f32[1,80,1024]{2,1,0:T(8,128)S(1)} %get-tuple-element.49.refs_2_), custom_call_target="tpu_custom_call", output_to_operand_aliasing={{}: (2, {})} | custom-call | flops 536870912 | bytes 1048576 | tf_op jit(solution)/shard_map/attend/pallas_call | solution.py:172
  74.0 0.0 collective-permute-done.9.other_ref
  74.0 0.5 join.1
  74.5 12.3 %all_to_all.16.in_ref = bf16[16,3,32,128]{3,2,1,0:T(8,128)(2,1)S(1)} all-to-all(bf16[16,3,32,128]{3,2,1,0:T(8,128)(2,1)S(1)} %join.1), channel_id=1, replica_groups=mesh['zl'=4,'core'=2,'y'=4,'zh'=2,'x'=4] {'y','x'}, dimensions={0} | all-to-all | bytes 786432 | tf_op jit(solution)/shard_map/all_to_all | solution.py:399
  86.8 0.1 patch_sum.1
  86.9 10.7 %all_to_all.17.own_ref = bf16[8,3,16,128]{3,2,1,0:T(8,128)(2,1)S(1)} all-to-all(bf16[8,3,16,128]{3,2,1,0:T(8,128)(2,1)S(1)} %patch_sum.1), channel_id=1, replica_groups=mesh['zl'=4,'core'=2,'y'=4,'zh'=2,'x'=4] {'zl','zh'}, dimensions={0} | all-to-all | bytes 196608 | tf_op jit(solution)/shard_map/all_to_all | solution.py:399
  97.7 3.0 %collective-permute-start.10 = (bf16[8,3,16,128]{3,2,1,0:T(8,128)(2,1)S(1)}, bf16[8,3,16,128]{3,2,1,0:T(8,128)(2,1)S(1)}, u32[]{:S(2)}, u32[]{:S(2)}) collective-permute-start(bf16[8,3,16,128]{3,2,1,0:T(8,128)(2,1)S(1)} %all_to_all.17.own_ref), channel_id=1, source_target_pairs={{0,32},{32,0},{1,33},{33,1},{2,34},{34,2},{3,35},{35,3},{4,36},{36... | collective-permute-start | bytes 294920 | tf_op jit(solution)/shard_map/ppermute | solution.py:407
  100.6 0.9 collective-permute-done.10.other_ref
  101.6 0.0 copy-done
  101.6 0.0 copy-done.1
  101.6 0.0 copy-done.3
  101.6 4.3 %decode.1 = bf16[2,32,4,4,256]{4,3,2,1,0:T(4,128)(2,1)} custom-call(s32[2]{0:T(128)S(1)} %pad_add_fusion.where_ref, bf16[8,3,16,128]{3,2,1,0:T(8,128)(2,1)S(1)} %all_to_all.17.own_ref, bf16[8,3,16,128]{3,2,1,0:T(8,128)(2,1)S(1)} %collective-permute-done.10.other_ref, bf16[3,3,3,16,256]{4,3,2,1,0:T(8,128)(2,1)S(1)} %copy-done.1, f32[1,256]{1,0:T(1,128)S(1)} %bitcast.18, ...), custom_call_target="tpu_custom_call" | custom-call | flops 2147483648 | bytes 10485760 | tf_op jit(solution)/shard_map/decode/pallas_call | solution.py:373
  (3 shorter events, 0.0 us)
Async XLA Ops:
  21.8 4.1 %collective-permute-start = (bf16[16,96,128]{2,1,0:T(8,128)(2,1)S(1)}, bf16[16,96,128]{2,1,0:T(8,128)(2,1)S(1)}, u32[]{:S(2)}, u32[]{:S(2)}) collective-permute-start(bf16[16,96,128]{2,1,0:T(8,128)(2,1)S(1)} %slice.16.refs_1_), channel_id=1, source_target_pairs={{0,32},{32,0},{1,33},{33,1},{2,34},{34,2},{3,35},{35,3},{4,36},{36... | collective-permute-start | bytes 1179656 | tf_op jit(solution)/shard_map/ppermute | solution.py:407
  24.0 3.5 %collective-permute-start.2 = (bf16[1024,128]{1,0:T(8,128)(2,1)S(1)}, bf16[1024,128]{1,0:T(8,128)(2,1)S(1)}, u32[]{:S(2)}, u32[]{:S(2)}) collective-permute-start(bf16[1024,128]{1,0:T(8,128)(2,1)S(1)} %bitcast.12), channel_id=1, source_target_pairs={{0,32},{32,0},{1,33},{33,1},{2,34},{34,2},{3,35},{35,3},{4,36},{36... | collective-permute-start | bytes 786440 | tf_op jit(solution)/shard_map/ppermute | solution.py:407
  24.1 10.8 %collective-permute-start.3 = (bf16[16,96,128]{2,1,0:T(8,128)(2,1)S(1)}, bf16[16,96,128]{2,1,0:T(8,128)(2,1)S(1)}, u32[]{:S(2)}, u32[]{:S(2)}) collective-permute-start(bf16[16,96,128]{2,1,0:T(8,128)(2,1)S(1)} %slice.16.refs_1_), channel_id=1, source_target_pairs={{0,196},{64,0},{128,64},{192,128},{4,192},{68,4},{132,68},{196,132... | collective-permute-start | bytes 1179656 | tf_op jit(solution)/shard_map/ppermute | solution.py:403
  25.9 13.2 %collective-permute-start.1 = (bf16[16,96,128]{2,1,0:T(8,128)(2,1)S(1)}, bf16[16,96,128]{2,1,0:T(8,128)(2,1)S(1)}, u32[]{:S(2)}, u32[]{:S(2)}) collective-permute-start(bf16[16,96,128]{2,1,0:T(8,128)(2,1)S(1)} %collective-permute-done), channel_id=1, source_target_pairs={{0,196},{64,0},{128,64},{192,128},{4,192},{68,4},{132,68},{196,132... | collective-permute-start | bytes 1179656 | tf_op jit(solution)/shard_map/ppermute | solution.py:403
  34.9 16.6 %collective-permute-start.5 = (bf16[16,96,128]{2,1,0:T(8,128)(2,1)S(1)}, bf16[16,96,128]{2,1,0:T(8,128)(2,1)S(1)}, u32[]{:S(2)}, u32[]{:S(2)}) collective-permute-start(bf16[16,96,128]{2,1,0:T(8,128)(2,1)S(1)} %collective-permute-done.3.refs_1_), channel_id=1, source_target_pairs={{0,196},{64,0},{128,64},{192,128},{4,192},{68,4},{132,68},{196,132... | collective-permute-start | bytes 1179656 | tf_op jit(solution)/shard_map/ppermute | solution.py:403
  39.1 16.6 %collective-permute-start.4 = (bf16[16,96,128]{2,1,0:T(8,128)(2,1)S(1)}, bf16[16,96,128]{2,1,0:T(8,128)(2,1)S(1)}, u32[]{:S(2)}, u32[]{:S(2)}) collective-permute-start(bf16[16,96,128]{2,1,0:T(8,128)(2,1)S(1)} %collective-permute-done.1.refs_1_), channel_id=1, source_target_pairs={{0,196},{64,0},{128,64},{192,128},{4,192},{68,4},{132,68},{196,132... | collective-permute-start | bytes 1179656 | tf_op jit(solution)/shard_map/ppermute | solution.py:403
  51.5 8.4 %collective-permute-start.7 = (bf16[16,96,128]{2,1,0:T(8,128)(2,1)S(1)}, bf16[16,96,128]{2,1,0:T(8,128)(2,1)S(1)}, u32[]{:S(2)}, u32[]{:S(2)}) collective-permute-start(bf16[16,96,128]{2,1,0:T(8,128)(2,1)S(1)} %collective-permute-done.5.refs_1_), channel_id=1, source_target_pairs={{0,196},{64,0},{128,64},{192,128},{4,192},{68,4},{132,68},{196,132... | collective-permute-start | bytes 1179656 | tf_op jit(solution)/shard_map/ppermute | solution.py:403
  55.7 8.4 %collective-permute-start.6 = (bf16[16,96,128]{2,1,0:T(8,128)(2,1)S(1)}, bf16[16,96,128]{2,1,0:T(8,128)(2,1)S(1)}, u32[]{:S(2)}, u32[]{:S(2)}) collective-permute-start(bf16[16,96,128]{2,1,0:T(8,128)(2,1)S(1)} %collective-permute-done.4.refs_1_), channel_id=1, source_target_pairs={{0,196},{64,0},{128,64},{192,128},{4,192},{68,4},{132,68},{196,132... | collective-permute-start | bytes 1179656 | tf_op jit(solution)/shard_map/ppermute | solution.py:403
  59.9 8.4 %collective-permute-start.8 = (bf16[16,96,128]{2,1,0:T(8,128)(2,1)S(1)}, bf16[16,96,128]{2,1,0:T(8,128)(2,1)S(1)}, u32[]{:S(2)}, u32[]{:S(2)}) collective-permute-start(bf16[16,96,128]{2,1,0:T(8,128)(2,1)S(1)} %collective-permute-done.7.refs_1_), channel_id=1, source_target_pairs={{0,196},{64,0},{128,64},{192,128},{4,192},{68,4},{132,68},{196,132... | collective-permute-start | bytes 1179656 | tf_op jit(solution)/shard_map/ppermute | solution.py:403
  68.4 33.1 %copy-start = (bf16[3,3,3,256,256]{4,3,2,1,0:T(8,128)(2,1)S(1)}, bf16[3,3,3,256,256]{4,3,2,1,0:T(8,128)(2,1)}, u32[]{:S(2)}) copy-start(bf16[3,3,3,256,256]{4,3,2,1,0:T(8,128)(2,1)} %w_out_ref.1) | copy-start | bytes 10616836
  68.4 33.1 %copy-start.1 = (bf16[3,3,3,16,256]{4,3,2,1,0:T(8,128)(2,1)S(1)}, bf16[3,3,3,16,256]{4,3,2,1,0:T(8,128)(2,1)}, u32[]{:S(2)}) copy-start(bf16[3,3,3,16,256]{4,3,2,1,0:T(8,128)(2,1)} %w_in_ref.1) | copy-start | bytes 663556
  68.5 33.1 %copy-start.2 = (f32[256]{0:T(256)S(1)}, f32[256]{0:T(256)}, u32[]{:S(2)}) copy-start(f32[256]{0:T(256)} %param.13) | copy-start | bytes 3076
  68.5 33.1 %copy-start.3 = (f32[256]{0:T(256)S(1)}, f32[256]{0:T(256)}, u32[]{:S(2)}) copy-start(f32[256]{0:T(256)} %param.15) | copy-start | bytes 3076
  69.7 4.3 %collective-permute-start.9 = (f32[80,1024]{1,0:T(8,128)S(1)}, f32[80,1024]{1,0:T(8,128)S(1)}, u32[]{:S(2)}, u32[]{:S(2)}) collective-permute-start(f32[80,1024]{1,0:T(8,128)S(1)} %bitcast.15), channel_id=1, source_target_pairs={{0,32},{32,0},{1,33},{33,1},{2,34},{34,2},{3,35},{35,3},{4,36},{36... | collective-permute-start | bytes 983048 | tf_op jit(solution)/shard_map/ppermute | solution.py:407
  97.7 3.9 %collective-permute-start.10 = (bf16[8,3,16,128]{3,2,1,0:T(8,128)(2,1)S(1)}, bf16[8,3,16,128]{3,2,1,0:T(8,128)(2,1)S(1)}, u32[]{:S(2)}, u32[]{:S(2)}) collective-permute-start(bf16[8,3,16,128]{3,2,1,0:T(8,128)(2,1)S(1)} %all_to_all.17.own_ref), channel_id=1, source_target_pairs={{0,32},{32,0},{1,33},{33,1},{2,34},{34,2},{3,35},{35,3},{4,36},{36... | collective-permute-start | bytes 294920 | tf_op jit(solution)/shard_map/ppermute | solution.py:407

commit v3 on v2

--- a/solution.py
+++ b/solution.py
@@ -415,8 +415,10 @@
     mine = mixed[:, 0:MSG]
     own_q = mixed[:, MSG:].reshape(PLANE_TOK, HD)
     both_q = jnp.stack([own_q, across(own_q)])
-    state = attend(both_q, mine, None)
-    coming = [hop(mine), hop(across(mine))]
+    state = attend(both_q, mine[0:8], None)
+    other, state = lax.optimization_barrier((across(mine), state))
+    coming = [hop(mine), hop(other)]
+    state = attend(both_q, mine[8:16], state)
     for step in range(6):
         message, state, where = lax.optimization_barrier((coming.pop(0), state, where))
         if step < 5:

time: 106 us -> 101 us (0.953)
  waiting for transfers between devices: 21.9 us -> 15.2 us
  starting transfers between devices: 12.5 us -> 14.1 us
    ppermute x7, waiting for transfers between devices: 20.9 us -> 14.2 us  [hop(): return lax.ppermute(value, STACK, around())]
    pallas_call x9 -> x10, Pallas kernels: 21.4 us -> 22 us  [attend(): pl.pallas_call(functools.partial(attend_kernel, first), out_shape=jax.Sha...]
  transfers between devices with their start and end apart: 11 -> 11, of which waited for: 8 -> 8; matrix products, arithmetic and copies ran while one was open for 0% -> 0% of each run, Pallas kernels for 19% -> 20%
where the time goes in v3:
time: 101 us
  blocking collectives  42.4 us (42%)
  Pallas kernels  29.2 us (29%)
  waiting for transfers between devices  15.2 us (15%)
  starting transfers between devices  14.1 us (14%)
    all_to_all x3, blocking collectives, swapped(): return lax.all_to_all(value, axes, split_axis=0, concat_axis=0, tiled=True)  42.4 us
    pallas_call x10, Pallas kernels, attend(): pl.pallas_call(functools.partial(attend_kernel, first), out_shape=jax.Sha...  22 us
    ppermute x7, waiting for transfers between devices, hop(): return lax.ppermute(value, STACK, around())  14.2 us
    ppermute x4, starting transfers between devices, across(): return lax.ppermute(value, 'core', [(0, 1), (1, 0)])  8.79 us
    ppermute x7, starting transfers between devices, hop(): return lax.ppermute(value, STACK, around())  5.26 us
    pallas_call x1, Pallas kernels, decode(): pl.pallas_call(decode_kernel, in_specs=[pl.BlockSpec(memory_space=pltpu.S...  4.29 us
    pallas_call x1, Pallas kernels, pack(): pl.pallas_call(pack_kernel, in_specs=[pl.BlockSpec(memory_space=pl.ANY)]...  2.34 us
  transfers between devices with their start and end apart: 11, of which 8 were waited for; matrix products, arithmetic and copies ran while one was open for 0% of the time, Pallas kernels for 20%

profile of v3, /device:TPU:1, one launch (start us, length us, event | category | flops | bytes accessed | tf_op | source)
XLA Modules:
  0.0 101.3 jit_solution(12532345649497850297)
XLA Ops:
  0.0 2.3 %pack.1 = bf16[16,160,128]{2,1,0:T(8,128)(2,1)} custom-call(bf16[64,2048]{1,0:T(8,128)(2,1)} %q_hbm.1, bf16[64,2048]{1,0:T(8,128)(2,1)} %k_hbm.1, bf16[64,2048]{1,0:T(8,128)(2,1)} %v_hbm.1, bf16[64,2048]{1,0:T(8,128)(2,1)} %bitcast.20), custom_call_target="tpu_custom_call" | custom-call | flops 16777216 | bytes 1048576 | tf_op jit(solution)/shard_map/pack/pallas_call | solution.py:64
  2.4 19.4 %all_to_all.15 = bf16[16,160,128]{2,1,0:T(8,128)(2,1)S(1)} all-to-all(bf16[16,160,128]{2,1,0:T(8,128)(2,1)} %pack.1), channel_id=1, replica_groups=mesh['zl'=4,'core'=2,'y'=4,'zh'=2,'x'=4] {'y','x'}, dimensions={0} | all-to-all | bytes 1310720 | tf_op jit(solution)/shard_map/all_to_all | solution.py:399
  21.8 2.2 %collective-permute-start.1 = (bf16[1024,128]{1,0:T(8,128)(2,1)S(1)}, bf16[1024,128]{1,0:T(8,128)(2,1)S(1)}, u32[]{:S(2)}, u32[]{:S(2)}) collective-permute-start(bf16[1024,128]{1,0:T(8,128)(2,1)S(1)} %bitcast.12), channel_id=1, source_target_pairs={{0,32},{32,0},{1,33},{33,1},{2,34},{34,2},{3,35},{35,3},{4,36},{36... | collective-permute-start | bytes 786440 | tf_op jit(solution)/shard_map/ppermute | solution.py:407
  24.0 0.1 collective-permute-start
  24.1 1.7 %collective-permute-start.3 = (bf16[16,96,128]{2,1,0:T(8,128)(2,1)S(1)}, bf16[16,96,128]{2,1,0:T(8,128)(2,1)S(1)}, u32[]{:S(2)}, u32[]{:S(2)}) collective-permute-start(bf16[16,96,128]{2,1,0:T(8,128)(2,1)S(1)} %slice.26), channel_id=1, source_target_pairs={{0,196},{64,0},{128,64},{192,128},{4,192},{68,4},{132,68},{196,132... | collective-permute-start | bytes 1179656 | tf_op jit(solution)/shard_map/ppermute | solution.py:403
  25.8 0.0 collective-permute-done.1
  25.8 0.1 pad_maximum_fusion.refs_0_
  25.9 3.5 %attend.10.refs_2_ = f32[2,80,1024]{2,1,0:T(8,128)S(1)} custom-call(bf16[2,1024,128]{2,1,0:T(8,128)(2,1)S(1)} %pad_maximum_fusion.refs_0_, bf16[8,96,128]{2,1,0:T(8,128)(2,1)S(1)} %get-tuple-element.58.refs_1_), custom_call_target="tpu_custom_call" | custom-call | flops 536870912 | bytes 2097152 | tf_op jit(solution)/shard_map/attend/pallas_call | solution.py:172
  29.4 0.0 collective-permute-done
  29.4 1.7 %collective-permute-start.2 = (bf16[16,96,128]{2,1,0:T(8,128)(2,1)S(1)}, bf16[16,96,128]{2,1,0:T(8,128)(2,1)S(1)}, u32[]{:S(2)}, u32[]{:S(2)}) collective-permute-start(bf16[16,96,128]{2,1,0:T(8,128)(2,1)S(1)} %collective-permute-done), channel_id=1, source_target_pairs={{0,196},{64,0},{128,64},{192,128},{4,192},{68,4},{132,68},{196,132... | collective-permute-start | bytes 1179656 | tf_op jit(solution)/shard_map/ppermute | solution.py:403
  31.1 0.1 pad_add_fusion.where_ref
  31.2 1.5 %attend.11.refs_2_ = f32[2,80,1024]{2,1,0:T(8,128)S(1)} custom-call(bf16[2,1024,128]{2,1,0:T(8,128)(2,1)S(1)} %pad_maximum_fusion.refs_0_, bf16[8,96,128]{2,1,0:T(8,128)(2,1)S(1)} %get-tuple-element.57.refs_1_, f32[2,80,1024]{2,1,0:T(8,128)S(1)} %attend.10.refs_2_), custom_call_target="tpu_custom_call", output_to_operand_aliasing={{}: (2, {})} | custom-call | flops 536870912 | bytes 2097152 | tf_op jit(solution)/shard_map/attend/pallas_call | solution.py:172
  32.7 2.2 %collective-permute-done.3.refs_1_ = bf16[16,96,128]{2,1,0:T(8,128)(2,1)S(1)} collective-permute-done((bf16[16,96,128]{2,1,0:T(8,128)(2,1)S(1)}, bf16[16,96,128]{2,1,0:T(8,128)(2,1)S(1)}, u32[]{:S(2)}, u32[]{:S(2)}) %collective-permute-start.3) | collective-permute-done | bytes 393248 | tf_op jit(solution)/shard_map/ppermute | solution.py:403
  34.9 0.0 collective-permute-start.5
  34.9 2.4 %attend.12.refs_2_ = f32[2,80,1024]{2,1,0:T(8,128)S(1)} custom-call(bf16[2,1024,128]{2,1,0:T(8,128)(2,1)S(1)} %pad_maximum_fusion.refs_0_, bf16[16,96,128]{2,1,0:T(8,128)(2,1)S(1)} %collective-permute-done.3.refs_1_, f32[2,80,1024]{2,1,0:T(8,128)S(1)} %attend.11.refs_2_), custom_call_target="tpu_custom_call", output_to_operand_aliasing={{}: (2, {})} | custom-call | flops 1073741824 | bytes 2097152 | tf_op jit(solution)/shard_map/attend/pallas_call | solution.py:172
  37.3 2.2 %collective-permute-done.2.refs_1_ = bf16[16,96,128]{2,1,0:T(8,128)(2,1)S(1)} collective-permute-done((bf16[16,96,128]{2,1,0:T(8,128)(2,1)S(1)}, bf16[16,96,128]{2,1,0:T(8,128)(2,1)S(1)}, u32[]{:S(2)}, u32[]{:S(2)}) %collective-permute-start.2) | collective-permute-done | bytes 393248 | tf_op jit(solution)/shard_map/ppermute | solution.py:403
  39.5 0.3 collective-permute-start.4
  39.8 2.4 %attend.13.refs_2_ = f32[2,80,1024]{2,1,0:T(8,128)S(1)} custom-call(bf16[2,1024,128]{2,1,0:T(8,128)(2,1)S(1)} %pad_maximum_fusion.refs_0_, bf16[16,96,128]{2,1,0:T(8,128)(2,1)S(1)} %collective-permute-done.2.refs_1_, f32[2,80,1024]{2,1,0:T(8,128)S(1)} %attend.12.refs_2_), custom_call_target="tpu_custom_call", output_to_operand_aliasing={{}: (2, {})} | custom-call | flops 1073741824 | bytes 2097152 | tf_op jit(solution)/shard_map/attend/pallas_call | solution.py:172
  42.2 4.3 %collective-permute-done.5.refs_1_ = bf16[16,96,128]{2,1,0:T(8,128)(2,1)S(1)} collective-permute-done((bf16[16,96,128]{2,1,0:T(8,128)(2,1)S(1)}, bf16[16,96,128]{2,1,0:T(8,128)(2,1)S(1)}, u32[]{:S(2)}, u32[]{:S(2)}) %collective-permute-start.5) | collective-permute-done | bytes 393248 | tf_op jit(solution)/shard_map/ppermute | solution.py:403
  46.5 0.0 collective-permute-start.7
  46.5 2.4 %attend.14.refs_2_ = f32[2,80,1024]{2,1,0:T(8,128)S(1)} custom-call(bf16[2,1024,128]{2,1,0:T(8,128)(2,1)S(1)} %pad_maximum_fusion.refs_0_, bf16[16,96,128]{2,1,0:T(8,128)(2,1)S(1)} %collective-permute-done.5.refs_1_, f32[2,80,1024]{2,1,0:T(8,128)S(1)} %attend.13.refs_2_), custom_call_target="tpu_custom_call", output_to_operand_aliasing={{}: (2, {})} | custom-call | flops 1073741824 | bytes 2097152 | tf_op jit(solution)/shard_map/attend/pallas_call | solution.py:172
  48.9 1.8 %collective-permute-done.4.refs_1_ = bf16[16,96,128]{2,1,0:T(8,128)(2,1)S(1)} collective-permute-done((bf16[16,96,128]{2,1,0:T(8,128)(2,1)S(1)}, bf16[16,96,128]{2,1,0:T(8,128)(2,1)S(1)}, u32[]{:S(2)}, u32[]{:S(2)}) %collective-permute-start.4) | collective-permute-done | bytes 393248 | tf_op jit(solution)/shard_map/ppermute | solution.py:403
  50.7 1.3 %collective-permute-start.6 = (bf16[16,96,128]{2,1,0:T(8,128)(2,1)S(1)}, bf16[16,96,128]{2,1,0:T(8,128)(2,1)S(1)}, u32[]{:S(2)}, u32[]{:S(2)}) collective-permute-start(bf16[16,96,128]{2,1,0:T(8,128)(2,1)S(1)} %collective-permute-done.4.refs_1_), channel_id=1, source_target_pairs={{0,196},{64,0},{128,64},{192,128},{4,192},{68,4},{132,68},{196,132... | collective-permute-start | bytes 1179656 | tf_op jit(solution)/shard_map/ppermute | solution.py:403
  52.0 2.4 %attend.15.refs_2_ = f32[2,80,1024]{2,1,0:T(8,128)S(1)} custom-call(bf16[2,1024,128]{2,1,0:T(8,128)(2,1)S(1)} %pad_maximum_fusion.refs_0_, bf16[16,96,128]{2,1,0:T(8,128)(2,1)S(1)} %collective-permute-done.4.refs_1_, f32[2,80,1024]{2,1,0:T(8,128)S(1)} %attend.14.refs_2_), custom_call_target="tpu_custom_call", output_to_operand_aliasing={{}: (2, {})} | custom-call | flops 1073741824 | bytes 2097152 | tf_op jit(solution)/shard_map/attend/pallas_call | solution.py:172
  54.4 0.5 collective-permute-done.7.refs_1_
  54.9 0.3 collective-permute-start.8
  55.2 2.4 %attend.16.refs_2_ = f32[2,80,1024]{2,1,0:T(8,128)S(1)} custom-call(bf16[2,1024,128]{2,1,0:T(8,128)(2,1)S(1)} %pad_maximum_fusion.refs_0_, bf16[16,96,128]{2,1,0:T(8,128)(2,1)S(1)} %collective-permute-done.7.refs_1_, f32[2,80,1024]{2,1,0:T(8,128)S(1)} %attend.15.refs_2_), custom_call_target="tpu_custom_call", output_to_operand_aliasing={{}: (2, {})} | custom-call | flops 1073741824 | bytes 2097152 | tf_op jit(solution)/shard_map/attend/pallas_call | solution.py:172
  57.6 1.5 %collective-permute-done.6.refs_1_ = bf16[16,96,128]{2,1,0:T(8,128)(2,1)S(1)} collective-permute-done((bf16[16,96,128]{2,1,0:T(8,128)(2,1)S(1)}, bf16[16,96,128]{2,1,0:T(8,128)(2,1)S(1)}, u32[]{:S(2)}, u32[]{:S(2)}) %collective-permute-start.6) | collective-permute-done | bytes 393248 | tf_op jit(solution)/shard_map/ppermute | solution.py:403
  59.1 2.4 %attend.17 = f32[2,80,1024]{2,1,0:T(8,128)S(1)} custom-call(bf16[2,1024,128]{2,1,0:T(8,128)(2,1)S(1)} %pad_maximum_fusion.refs_0_, bf16[16,96,128]{2,1,0:T(8,128)(2,1)S(1)} %collective-permute-done.6.refs_1_, f32[2,80,1024]{2,1,0:T(8,128)S(1)} %attend.16.refs_2_), custom_call_target="tpu_custom_call", output_to_operand_aliasing={{}: (2, {})} | custom-call | flops 1073741824 | bytes 2097152 | tf_op jit(solution)/shard_map/attend/pallas_call | solution.py:172
  61.5 1.8 %collective-permute-done.8.refs_1_ = bf16[16,96,128]{2,1,0:T(8,128)(2,1)S(1)} collective-permute-done((bf16[16,96,128]{2,1,0:T(8,128)(2,1)S(1)}, bf16[16,96,128]{2,1,0:T(8,128)(2,1)S(1)}, u32[]{:S(2)}, u32[]{:S(2)}) %collective-permute-start.8) | collective-permute-done | bytes 393248 | tf_op jit(solution)/shard_map/ppermute | solution.py:403
  63.3 0.1 fusion
  63.4 0.0 copy-start
  63.4 0.0 copy-start.1
  63.4 0.0 copy-start.2
  63.4 0.0 copy-start.3
  63.4 1.2 %attend.18 = f32[1,80,1024]{2,1,0:T(8,128)S(1)} custom-call(bf16[1,1024,128]{2,1,0:T(8,128)(2,1)S(1)} %bitcast.17, bf16[16,96,128]{2,1,0:T(8,128)(2,1)S(1)} %collective-permute-done.8.refs_1_, f32[1,80,1024]{2,1,0:T(8,128)S(1)} %get-tuple-element.56.refs_2_), custom_call_target="tpu_custom_call", output_to_operand_aliasing={{}: (2, {})} | custom-call | flops 536870912 | bytes 1048576 | tf_op jit(solution)/shard_map/attend/pallas_call | solution.py:172
  64.7 3.5 %collective-permute-start.9 = (f32[80,1024]{1,0:T(8,128)S(1)}, f32[80,1024]{1,0:T(8,128)S(1)}, u32[]{:S(2)}, u32[]{:S(2)}) collective-permute-start(f32[80,1024]{1,0:T(8,128)S(1)} %bitcast.15), channel_id=1, source_target_pairs={{0,32},{32,0},{1,33},{33,1},{2,34},{34,2},{3,35},{35,3},{4,36},{36... | collective-permute-start | bytes 983048 | tf_op jit(solution)/shard_map/ppermute | solution.py:407
  68.2 1.2 %attend.19 = f32[1,80,1024]{2,1,0:T(8,128)S(1)} custom-call(bf16[1,1024,128]{2,1,0:T(8,128)(2,1)S(1)} %bitcast.14, bf16[16,96,128]{2,1,0:T(8,128)(2,1)S(1)} %collective-permute-done.8.refs_1_, f32[1,80,1024]{2,1,0:T(8,128)S(1)} %get-tuple-element.53.refs_2_), custom_call_target="tpu_custom_call", output_to_operand_aliasing={{}: (2, {})} | custom-call | flops 536870912 | bytes 1048576 | tf_op jit(solution)/shard_map/attend/pallas_call | solution.py:172
  69.4 0.0 collective-permute-done.9.other_ref
  69.5 0.5 join.1
  69.9 12.3 %all_to_all.16.in_ref = bf16[16,3,32,128]{3,2,1,0:T(8,128)(2,1)S(1)} all-to-all(bf16[16,3,32,128]{3,2,1,0:T(8,128)(2,1)S(1)} %join.1), channel_id=1, replica_groups=mesh['zl'=4,'core'=2,'y'=4,'zh'=2,'x'=4] {'y','x'}, dimensions={0} | all-to-all | bytes 786432 | tf_op jit(solution)/shard_map/all_to_all | solution.py:399
  82.3 0.1 patch_sum.1
  82.4 10.7 %all_to_all.17.own_ref = bf16[8,3,16,128]{3,2,1,0:T(8,128)(2,1)S(1)} all-to-all(bf16[8,3,16,128]{3,2,1,0:T(8,128)(2,1)S(1)} %patch_sum.1), channel_id=1, replica_groups=mesh['zl'=4,'core'=2,'y'=4,'zh'=2,'x'=4] {'zl','zh'}, dimensions={0} | all-to-all | bytes 196608 | tf_op jit(solution)/shard_map/all_to_all | solution.py:399
  93.1 3.0 %collective-permute-start.10 = (bf16[8,3,16,128]{3,2,1,0:T(8,128)(2,1)S(1)}, bf16[8,3,16,128]{3,2,1,0:T(8,128)(2,1)S(1)}, u32[]{:S(2)}, u32[]{:S(2)}) collective-permute-start(bf16[8,3,16,128]{3,2,1,0:T(8,128)(2,1)S(1)} %all_to_all.17.own_ref), channel_id=1, source_target_pairs={{0,32},{32,0},{1,33},{33,1},{2,34},{34,2},{3,35},{35,3},{4,36},{36... | collective-permute-start | bytes 294920 | tf_op jit(solution)/shard_map/ppermute | solution.py:407
  96.1 0.9 collective-permute-done.10.other_ref
  97.0 0.0 copy-done
  97.0 0.0 copy-done.1
  97.0 4.3 %decode.1 = bf16[2,32,4,4,256]{4,3,2,1,0:T(4,128)(2,1)} custom-call(s32[2]{0:T(128)S(1)} %pad_add_fusion.where_ref, bf16[8,3,16,128]{3,2,1,0:T(8,128)(2,1)S(1)} %all_to_all.17.own_ref, bf16[8,3,16,128]{3,2,1,0:T(8,128)(2,1)S(1)} %collective-permute-done.10.other_ref, bf16[3,3,3,16,256]{4,3,2,1,0:T(8,128)(2,1)S(1)} %copy-done.1, f32[1,256]{1,0:T(1,128)S(1)} %bitcast.18, ...), custom_call_target="tpu_custom_call" | custom-call | flops 2147483648 | bytes 10485760 | tf_op jit(solution)/shard_map/decode/pallas_call | solution.py:373
  (5 shorter events, 0.1 us)
Async XLA Ops:
  21.8 4.1 %collective-permute-start.1 = (bf16[1024,128]{1,0:T(8,128)(2,1)S(1)}, bf16[1024,128]{1,0:T(8,128)(2,1)S(1)}, u32[]{:S(2)}, u32[]{:S(2)}) collective-permute-start(bf16[1024,128]{1,0:T(8,128)(2,1)S(1)} %bitcast.12), channel_id=1, source_target_pairs={{0,32},{32,0},{1,33},{33,1},{2,34},{34,2},{3,35},{35,3},{4,36},{36... | collective-permute-start | bytes 786440 | tf_op jit(solution)/shard_map/ppermute | solution.py:407
  24.0 5.4 %collective-permute-start = (bf16[16,96,128]{2,1,0:T(8,128)(2,1)S(1)}, bf16[16,96,128]{2,1,0:T(8,128)(2,1)S(1)}, u32[]{:S(2)}, u32[]{:S(2)}) collective-permute-start(bf16[16,96,128]{2,1,0:T(8,128)(2,1)S(1)} %slice.26), channel_id=1, source_target_pairs={{0,32},{32,0},{1,33},{33,1},{2,34},{34,2},{3,35},{35,3},{4,36},{36... | collective-permute-start | bytes 1179656 | tf_op jit(solution)/shard_map/ppermute | solution.py:407
  24.1 10.8 %collective-permute-start.3 = (bf16[16,96,128]{2,1,0:T(8,128)(2,1)S(1)}, bf16[16,96,128]{2,1,0:T(8,128)(2,1)S(1)}, u32[]{:S(2)}, u32[]{:S(2)}) collective-permute-start(bf16[16,96,128]{2,1,0:T(8,128)(2,1)S(1)} %slice.26), channel_id=1, source_target_pairs={{0,196},{64,0},{128,64},{192,128},{4,192},{68,4},{132,68},{196,132... | collective-permute-start | bytes 1179656 | tf_op jit(solution)/shard_map/ppermute | solution.py:403
  29.4 10.1 %collective-permute-start.2 = (bf16[16,96,128]{2,1,0:T(8,128)(2,1)S(1)}, bf16[16,96,128]{2,1,0:T(8,128)(2,1)S(1)}, u32[]{:S(2)}, u32[]{:S(2)}) collective-permute-start(bf16[16,96,128]{2,1,0:T(8,128)(2,1)S(1)} %collective-permute-done), channel_id=1, source_target_pairs={{0,196},{64,0},{128,64},{192,128},{4,192},{68,4},{132,68},{196,132... | collective-permute-start | bytes 1179656 | tf_op jit(solution)/shard_map/ppermute | solution.py:403
  34.9 11.6 %collective-permute-start.5 = (bf16[16,96,128]{2,1,0:T(8,128)(2,1)S(1)}, bf16[16,96,128]{2,1,0:T(8,128)(2,1)S(1)}, u32[]{:S(2)}, u32[]{:S(2)}) collective-permute-start(bf16[16,96,128]{2,1,0:T(8,128)(2,1)S(1)} %collective-permute-done.3.refs_1_), channel_id=1, source_target_pairs={{0,196},{64,0},{128,64},{192,128},{4,192},{68,4},{132,68},{196,132... | collective-permute-start | bytes 1179656 | tf_op jit(solution)/shard_map/ppermute | solution.py:403
  39.5 11.2 %collective-permute-start.4 = (bf16[16,96,128]{2,1,0:T(8,128)(2,1)S(1)}, bf16[16,96,128]{2,1,0:T(8,128)(2,1)S(1)}, u32[]{:S(2)}, u32[]{:S(2)}) collective-permute-start(bf16[16,96,128]{2,1,0:T(8,128)(2,1)S(1)} %collective-permute-done.2.refs_1_), channel_id=1, source_target_pairs={{0,196},{64,0},{128,64},{192,128},{4,192},{68,4},{132,68},{196,132... | collective-permute-start | bytes 1179656 | tf_op jit(solution)/shard_map/ppermute | solution.py:403
  46.5 8.4 %collective-permute-start.7 = (bf16[16,96,128]{2,1,0:T(8,128)(2,1)S(1)}, bf16[16,96,128]{2,1,0:T(8,128)(2,1)S(1)}, u32[]{:S(2)}, u32[]{:S(2)}) collective-permute-start(bf16[16,96,128]{2,1,0:T(8,128)(2,1)S(1)} %collective-permute-done.5.refs_1_), channel_id=1, source_target_pairs={{0,196},{64,0},{128,64},{192,128},{4,192},{68,4},{132,68},{196,132... | collective-permute-start | bytes 1179656 | tf_op jit(solution)/shard_map/ppermute | solution.py:403
  50.7 8.4 %collective-permute-start.6 = (bf16[16,96,128]{2,1,0:T(8,128)(2,1)S(1)}, bf16[16,96,128]{2,1,0:T(8,128)(2,1)S(1)}, u32[]{:S(2)}, u32[]{:S(2)}) collective-permute-start(bf16[16,96,128]{2,1,0:T(8,128)(2,1)S(1)} %collective-permute-done.4.refs_1_), channel_id=1, source_target_pairs={{0,196},{64,0},{128,64},{192,128},{4,192},{68,4},{132,68},{196,132... | collective-permute-start | bytes 1179656 | tf_op jit(solution)/shard_map/ppermute | solution.py:403
  54.9 8.4 %collective-permute-start.8 = (bf16[16,96,128]{2,1,0:T(8,128)(2,1)S(1)}, bf16[16,96,128]{2,1,0:T(8,128)(2,1)S(1)}, u32[]{:S(2)}, u32[]{:S(2)}) collective-permute-start(bf16[16,96,128]{2,1,0:T(8,128)(2,1)S(1)} %collective-permute-done.7.refs_1_), channel_id=1, source_target_pairs={{0,196},{64,0},{128,64},{192,128},{4,192},{68,4},{132,68},{196,132... | collective-permute-start | bytes 1179656 | tf_op jit(solution)/shard_map/ppermute | solution.py:403
  63.4 33.6 %copy-start = (bf16[3,3,3,256,256]{4,3,2,1,0:T(8,128)(2,1)S(1)}, bf16[3,3,3,256,256]{4,3,2,1,0:T(8,128)(2,1)}, u32[]{:S(2)}) copy-start(bf16[3,3,3,256,256]{4,3,2,1,0:T(8,128)(2,1)} %w_out_ref.1) | copy-start | bytes 10616836
  63.4 33.6 %copy-start.1 = (bf16[3,3,3,16,256]{4,3,2,1,0:T(8,128)(2,1)S(1)}, bf16[3,3,3,16,256]{4,3,2,1,0:T(8,128)(2,1)}, u32[]{:S(2)}) copy-start(bf16[3,3,3,16,256]{4,3,2,1,0:T(8,128)(2,1)} %w_in_ref.1) | copy-start | bytes 663556
  63.4 33.6 %copy-start.2 = (f32[256]{0:T(256)S(1)}, f32[256]{0:T(256)}, u32[]{:S(2)}) copy-start(f32[256]{0:T(256)} %param.13) | copy-start | bytes 3076
  63.4 33.6 %copy-start.3 = (f32[256]{0:T(256)S(1)}, f32[256]{0:T(256)}, u32[]{:S(2)}) copy-start(f32[256]{0:T(256)} %param.15) | copy-start | bytes 3076
  64.7 4.8 %collective-permute-start.9 = (f32[80,1024]{1,0:T(8,128)S(1)}, f32[80,1024]{1,0:T(8,128)S(1)}, u32[]{:S(2)}, u32[]{:S(2)}) collective-permute-start(f32[80,1024]{1,0:T(8,128)S(1)} %bitcast.15), channel_id=1, source_target_pairs={{0,32},{32,0},{1,33},{33,1},{2,34},{34,2},{3,35},{35,3},{4,36},{36... | collective-permute-start | bytes 983048 | tf_op jit(solution)/shard_map/ppermute | solution.py:407
  93.1 3.9 %collective-permute-start.10 = (bf16[8,3,16,128]{3,2,1,0:T(8,128)(2,1)S(1)}, bf16[8,3,16,128]{3,2,1,0:T(8,128)(2,1)S(1)}, u32[]{:S(2)}, u32[]{:S(2)}) collective-permute-start(bf16[8,3,16,128]{3,2,1,0:T(8,128)(2,1)S(1)} %all_to_all.17.own_ref), channel_id=1, source_target_pairs={{0,32},{32,0},{1,33},{33,1},{2,34},{34,2},{3,35},{35,3},{4,36},{36... | collective-permute-start | bytes 294920 | tf_op jit(solution)/shard_map/ppermute | solution.py:407
